TPU v7x, 256 devices: a whole 4x4x8 slice. The times are simulated.
256 devices in a mesh: aux: 32 (over x, z), occ: 8 (over y, core).
Axes of the slice: x: 4, y: 4, z: 8, core: 2. Of those that a mesh axis runs over, the one named last changes fastest.
Arguments:
- blocks: float32 [1536, 16, 4096], P('aux', 'occ'), may hold values from -6 to 6
- pair_list: int32 [32, 16, 2], P('aux', 'occ'), may hold values from 0 to 15
- pair_count: int32 [32], P('aux'), may hold values from 4 to 16, as said below
- orbitals: float32 [128, 1024], replicated, may hold values from -0.0009765625 to 0.0009765625
Outputs:
- exchange: float32 [1024, 1024], P('aux', 'occ')
Inputs may be any that keep to these rules, and one draw needn't show every extreme that they name: `pair_list`: block indices of the kept pairs; pairs may repeat. `pair_count`: slots at or beyond an auxiliary block's count are padding and contribute nothing; some auxiliary block uses all 16 slots.
All inputs are finite; a program needn't handle non-finite values.
Results may differ from a plain program's by a relative error of at most 0.0003.
Values sent between devices are 32-bit elements; how exact they have to be, the bound alone decides.
No kernel may reach another device: no remote copies, remote signals or barrier semaphores. Data moves between devices by JAX's collectives and lax.ppermute only.
A program may use at most 64 MiB of HBM per device.

v0:
```python
import jax
import jax.numpy as jnp
from jax import lax
from jax.sharding import PartitionSpec as P

NBF = 1024
BLK = 64


def copy_for_each(array, axis):
    devices = lax.axis_size(axis)
    return lax.all_to_all(
        jnp.broadcast_to(array[None], (devices, *array.shape)), axis, 0, 0, tiled=True
    )


def in_order(parts, dim):
    parts = jnp.moveaxis(parts, 0, dim)
    shape = parts.shape
    return parts.reshape(*shape[:dim], shape[dim] * shape[dim + 1], *shape[dim + 2 :])


def gathered_copies(array, axis, dim):
    parts = copy_for_each(array, axis)
    return in_order(parts, dim)


def split_up(array, dim, devices):
    before, after = (array.shape[:dim], array.shape[dim + 1 :])
    return jnp.moveaxis(array.reshape(*before, devices, -1, *after), dim, 0)


def sent_and_summed(array, axis, dim):
    devices = lax.axis_size(axis)
    parts = lax.all_to_all(split_up(array, dim, devices), axis, 0, 0, tiled=True)
    return jnp.sum(parts, axis=0)


def per_device(blocks, pair_list, pair_count, orbitals):
    aux_rows = blocks.shape[0]
    slot_count = blocks.shape[1]
    orbital_count = orbitals.shape[0]
    n_blocks = NBF // BLK
    occ_devs = lax.axis_size("occ")
    positions = jnp.arange(n_blocks, dtype=jnp.int32)
    first_slot = lax.axis_index("occ") * slot_count
    live_slot = first_slot + jnp.arange(slot_count, dtype=jnp.int32) < pair_count[0]
    row_ids = jnp.where(live_slot, pair_list[0, :, 0], -1)
    col_onehot = (pair_list[0, :, 1][:, None] == positions[None, :]).astype(jnp.float32)
    coefficients = orbitals.reshape(orbital_count, n_blocks, BLK)
    picked_cols = jnp.einsum(
        "iNn,sN->sin", coefficients, col_onehot, precision=lax.Precision.HIGHEST
    )
    tile_data = blocks.reshape(aux_rows, slot_count, BLK, BLK)
    half_tiles = jnp.einsum(
        "qsmn,sin->isqm", tile_data, picked_cols, precision=lax.Precision.HIGHEST
    )
    arrived = lax.all_to_all(
        half_tiles.reshape(orbital_count, slot_count, aux_rows * BLK),
        "occ",
        split_axis=0,
        concat_axis=1,
        tiled=True,
    )
    every_ids = gathered_copies(row_ids, "occ", 0)
    row_onehot = (every_ids[:, None] == positions[None, :]).astype(jnp.float32)
    owned_rows = arrived.reshape(orbital_count // occ_devs, slot_count * occ_devs, aux_rows, BLK)
    transformed = jnp.einsum(
        "isqm,sM->iqMm", owned_rows, row_onehot, precision=lax.Precision.HIGHEST
    )
    transformed = transformed.reshape(orbital_count // occ_devs * aux_rows, NBF)
    partial_value = jnp.einsum(
        "rm,rn->mn", transformed, transformed, precision=lax.Precision.HIGHEST
    )
    by_column = lax.psum_scatter(partial_value, "occ", scatter_dimension=1, tiled=True)
    result = sent_and_summed(by_column, "aux", 0)
    return result


def solution(mesh):
    in_specs = (P("aux", "occ", None), P("aux", "occ", None), P("aux"), P())
    out_specs = P("aux", "occ")
    return jax.shard_map(
        per_device, mesh=mesh, in_specs=in_specs, out_specs=out_specs, check_vma=False
    )
```

profile of v0, /device:TPU:8, one launch (start us, length us, event | category | flops | bytes accessed | tf_op | source)
XLA Modules:
  0.0 178.9 jit_solution(853255660558135233)
XLA Ops:
  7.2 1.0 slice_reduce_fusion.1
  8.2 0.6 broadcast_in_dim.7
  8.8 5.4 %all-to-all-start = ((s32[8,1,2]{2,1,0:T(1,128)}), s32[8,1,2]{2,1,0:T(1,128)S(1)}, u32[]{:S(2)}, u32[]{:S(2)}) async-start(s32[8,1,2]{2,1,0:T(1,128)} %broadcast_in_dim.7), calls=%async_computation | async-start | bytes 8192 | tf_op jit(solution)/shard_map/all_to_all | solution.py:12
  14.2 2.0 %copy.11 = f32[128,1024]{0,1:T(8,128)} copy(f32[128,1024]{1,0:T(8,128)} %param.7) | data formatting | bytes 1048576 | tf_op args[3]
  16.2 3.0 %reshape.39 = f32[48,2,64,64]{3,2,1,0:T(8,128)S(1)} reshape(f32[48,2,4096]{2,1,0:T(2,128)} %param.4) | data formatting | bytes 3145728 | tf_op jit(solution)/shard_map/reshape | solution.py:54
  19.2 1.6 convolution_bitcast_fusion
  20.9 4.4 %fusion.2 = f32[2,128,48,64]{1,3,2,0:T(8,128)} fusion(f32[48,2,64,64]{3,2,1,0:T(8,128)S(1)} %reshape.39, f32[2,128,64,1]{1,0,2,3:T(2,128)S(1)} %convolution_bitcast_fusion), kind=kOutput, calls=%fused_computation.2 | convolution fusion | flops 603979776 | bytes 4784128 | tf_op jit(solution)/shard_map/qsmn,sin->isqm/dot_general | solution.py:55
  25.2 5.9 %copy.15 = f32[128,2,3072]{2,1,0:T(2,128)} copy(f32[128,2,3072]{0,2,1:T(8,128)} %bitcast.30) | data formatting | bytes 6291456 | tf_op jit(solution)/shard_map/reshape | solution.py:59
  31.1 0.0 all-to-all-done
  31.1 4.8 %all-to-all-start.1 = ((f32[128,2,3072]{2,1,0:T(2,128)}), f32[128,2,3072]{2,1,0:T(2,128)S(1)}, u32[]{:S(2)}, u32[]{:S(2)}) async-start(f32[128,2,3072]{2,1,0:T(2,128)} %copy.15), calls=%async_computation.1 | async-start | bytes 6291456 | tf_op jit(solution)/shard_map/all_to_all | solution.py:58
  35.9 0.0 reduce-scatter.2.cloned.1.call-start
  35.9 0.5 broadcast.21
  36.4 0.7 reduce.7
  37.1 0.1 eq.30
  37.2 35.7 %all-to-all-done.1 = f32[128,2,3072]{2,1,0:T(2,128)S(1)} async-done(((f32[128,2,3072]{2,1,0:T(2,128)}), f32[128,2,3072]{2,1,0:T(2,128)S(1)}, u32[]{:S(2)}, u32[]{:S(2)}) %all-to-all-start.1) | async-done | bytes 3145760 | tf_op jit(solution)/shard_map/all_to_all | solution.py:58
  72.9 1.0 copy.16
  73.9 0.2 copy.17
  74.2 3.7 %reshape.41 = f32[16,16,48,64]{3,2,0,1:T(8,128)} reshape(f32[16,8,2,3072]{3,0,2,1:T(8,128)S(1)} %copy.17) | data formatting | bytes 6291456 | tf_op jit(solution)/shard_map/reshape | solution.py:67
  77.9 11.8 %fusion.4 = f32[16,48,16,64]{3,2,1,0:T(8,128)} fusion(f32[16,16,48,64]{3,2,0,1:T(8,128)} %reshape.41, s32[16]{0:T(128)S(1)} %eq.30), kind=kOutput, calls=%fused_computation.4 | convolution fusion | flops 150995200 | bytes 6291520 | tf_op jit(solution)/shard_map/isqm,sM->iqMm/dot_general | solution.py:68
  89.6 4.8 %reshape.42 = f32[768,1024]{1,0:T(8,128)S(1)} reshape(f32[16,48,16,64]{3,2,1,0:T(8,128)} %fusion.4) | data formatting | bytes 6291456 | tf_op jit(solution)/shard_map/reshape | solution.py:71
  94.5 11.7 %fusion.16 = f32[1024,1024]{1,0:T(8,128)} fusion(f32[768,1024]{1,0:T(8,128)S(1)} %reshape.42), kind=kOutput, calls=%fused_computation.18 | convolution fusion | flops 9663676416 | bytes 7340032 | tf_op jit(solution)/shard_map/rm,rn->mn/dot_general | solution.py:72
  106.2 0.0 reduce-scatter.2.cloned.1.call-update
  106.2 38.4 %reduce-scatter.2.cloned.1.call-done = f32[1024,128]{1,0:T(8,128)} async-done(((f32[1024,1024]{1,0:T(8,128)}), f32[1024,128]{1,0:T(8,128)}) %reduce-scatter.2.cloned.1.call-update) | async-done | bytes 524304 | tf_op jit(solution)/shard_map/reduce_scatter | solution.py:75
  144.6 26.8 %all_to_all.26 = f32[32,32,128]{2,1,0:T(8,128)S(1)} all-to-all(f32[32,32,128]{2,1,0:T(8,128)} %bitcast.33), channel_id=1, replica_groups=mesh['aux'=32,'occ'=8] {'aux'}, dimensions={0} | all-to-all | bytes 1048576 | tf_op jit(solution)/shard_map/all_to_all | solution.py:35
  171.4 0.6 reduce_sum.9
  (1 shorter events, 0.0 us)
Async XLA Ops:
  8.8 22.3 %all-to-all-start = ((s32[8,1,2]{2,1,0:T(1,128)}), s32[8,1,2]{2,1,0:T(1,128)S(1)}, u32[]{:S(2)}, u32[]{:S(2)}) async-start(s32[8,1,2]{2,1,0:T(1,128)} %broadcast_in_dim.7), calls=%async_computation | async-start | bytes 8192 | tf_op jit(solution)/shard_map/all_to_all | solution.py:12
  31.1 41.8 %all-to-all-start.1 = ((f32[128,2,3072]{2,1,0:T(2,128)}), f32[128,2,3072]{2,1,0:T(2,128)S(1)}, u32[]{:S(2)}, u32[]{:S(2)}) async-start(f32[128,2,3072]{2,1,0:T(2,128)} %copy.15), calls=%async_computation.1 | async-start | bytes 6291456 | tf_op jit(solution)/shard_map/all_to_all | solution.py:58
  35.9 108.7 %reduce-scatter.2.cloned.1.call-start = ((), (), s32[]{:S(2)}) async-start(), calls=%async_computation.4 | async-start | bytes 4718592 | tf_op jit(solution)/shard_map/reduce_scatter | solution.py:75
Sparse Core Ops, SparseCore 0:
  106.4 38.2 reduce-scatter.1
where the time goes:
time: 181 us; the launch traced here: 179 us
  waiting for transfers between devices  74.1 us (41%)
  matrix products  29.5 us (16%)
  blocking collectives  26.8 us (15%)
  local copies, waits for them, and re-layouts  22.9 us (13%)
  between operations  14.1 us (8%)
  starting transfers between devices  10.2 us (6%)
    reduce_scatter x1, waiting for transfers between devices, per_device(): lax.psum_scatter(partial_value, 'occ', scatter_dimension=1, tiled=True)  38.4 us
    all_to_all x1, waiting for transfers between devices, per_device(): lax.all_to_all(half_tiles.reshape(orbital_count, slot_count, aux_rows * B...  35.7 us
    all_to_all x1, blocking collectives, sent_and_summed(): lax.all_to_all(split_up(array, dim, devices), axis, 0, 0, tiled=True)  26.8 us
    dot_general x1, matrix products, per_device(): jnp.einsum('isqm,sM->iqMm', owned_rows, row_onehot, precision=lax.Precisi...  11.8 us
    dot_general x1, matrix products, per_device(): jnp.einsum('rm,rn->mn', transformed, transformed, precision=lax.Precision...  11.7 us
    reshape x1, local copies, waits for them, and re-layouts, per_device(): half_tiles.reshape(orbital_count, slot_count, aux_rows * BLK)  5.87 us
    all_to_all x1, starting transfers between devices, copy_for_each(): lax.all_to_all(jnp.broadcast_to(array[None], (devices, *array.shape)), ax...  5.4 us
    reshape x1, local copies, waits for them, and re-layouts, per_device(): transformed = transformed.reshape(orbital_count // occ_devs * aux_rows, NBF)  4.82 us
  transfers between devices with their start and end apart: 3, of which 2 were waited for; matrix products, arithmetic and copies ran while one was open for 10% of the time, Pallas kernels for 0%

commit v1 on v0

v1 whole, which is shorter than its diff:
```python
import functools

import jax
import jax.numpy as jnp
from jax import lax
from jax.experimental import pallas as pl
from jax.experimental.layout import Layout, with_layout_constraint
from jax.experimental.pallas import tpu as pltpu
from jax.sharding import PartitionSpec as P

NBF = 1024
BLK = 64
NOCC = 128
AUX_DEV = 48
NX, NZ, NY, NC = 4, 8, 4, 2
CHUNKS = (8, 4)
ROWS = BLK // 2
HEAD = 8
VMEM = pl.BlockSpec(memory_space=pltpu.VMEM)
SMEM = pl.BlockSpec(memory_space=pltpu.SMEM)
F32, BF16 = jnp.float32, jnp.bfloat16
NT = (((1,), (1,)), ((), ()))


def device_of(x, z, y, c):
    return ((x % NX) * NZ + z % NZ) * (NY * NC) + (y % NY) * NC + c % NC


def send(array, where):
    pairs = [
        (device_of(x, z, y, c), device_of(*where(x, z, y, c)))
        for x in range(NX)
        for z in range(NZ)
        for y in range(NY)
        for c in range(NC)
    ]
    return lax.ppermute(array, ("aux", "occ"), pairs)


def call(kernel, out_shape, in_specs, scratch=(), flops=0, bytes_accessed=0):
    return pl.pallas_call(
        kernel,
        out_shape=out_shape,
        in_specs=in_specs,
        out_specs=jax.tree.map(lambda _: VMEM, out_shape),
        scratch_shapes=list(scratch),
        compiler_params=pltpu.CompilerParams(vmem_limit_bytes=40 * 2**20),
        cost_estimate=pl.CostEstimate(
            flops=flops, bytes_accessed=bytes_accessed, transcendentals=0
        ),
    )


def split(values):
    high = values.astype(BF16)
    return high, (values - high.astype(F32)).astype(BF16)


def pack_kernel(info_ref, tiles_ref, *outs):
    lane = lax.broadcasted_iota(jnp.int32, (HEAD, 128), 1)
    head = jnp.zeros((HEAD, 128), F32)
    for j in range(6):
        head = jnp.where(lane == j, info_ref[1 + j].astype(F32), head)
    start = 0
    for chunk, count in enumerate(CHUNKS):
        for step in range(NY):
            out = outs[chunk * NY + step]
            chip = lax.rem(info_ref[0] + step, NY)
            base = (chip * (AUX_DEV // NY) + start) * BLK
            for slot in range(2):
                out[pl.ds(slot * count * ROWS, count * ROWS), :] = tiles_ref[
                    pl.ds(pl.multiple_of(base, 8) + slot, count * ROWS, stride=2), :
                ]
            if chunk == 0:
                out[pl.ds(2 * count * ROWS, HEAD), :] = head
        start += count


def weights_kernel(info_ref, orbitals_ref, both_ref, low_ref, high_t, low_t):
    high, low = split(orbitals_ref[...].T)
    high_t[...] = high
    low_t[...] = low
    zero = jnp.zeros((BLK, NOCC), BF16)
    for slot in range(16):
        column = pl.multiple_of(info_ref[slot, 1] * BLK, BLK)
        live = info_ref[slot, 2] > 0
        high = jnp.where(live, high_t[pl.ds(column, BLK), :].astype(F32), 0.0).astype(BF16)
        low = jnp.where(live, low_t[pl.ds(column, BLK), :].astype(F32), 0.0).astype(BF16)
        for half in range(2):
            both_ref[slot, pl.ds(half * 128, BLK), 0:128] = high
            both_ref[slot, pl.ds(half * 128, BLK), 128:256] = zero
            both_ref[slot, pl.ds(half * 128 + BLK, BLK), 0:128] = zero
            both_ref[slot, pl.ds(half * 128 + BLK, BLK), 128:256] = high
        low_ref[slot, 0:BLK, 0:128] = low
        low_ref[slot, 0:BLK, 128:256] = zero
        low_ref[slot, BLK:128, 0:128] = zero
        low_ref[slot, BLK:128, 128:256] = low


def product_kernel(count, first, last, info_ref, place_ref, both_ref, low_ref, *refs):
    payloads = refs[:8]
    refs = refs[8:]
    if not first:
        before, refs = refs[0], refs[1:]
    if last:
        outs, refs = refs[:4], refs[4:]
    else:
        outs, refs = refs[:1], refs[1:]
    half, high_ref, low_half_ref, total = refs
    y, x, core = place_ref[0], place_ref[1], place_ref[2]
    half[...] = jnp.zeros_like(half)
    for source in range(8):
        for slot in range(2):
            index = source * 2 + slot
            tiles = payloads[source][pl.ds(slot * count * ROWS, count * ROWS), :]
            high, low = split(tiles)
            part = jnp.dot(
                jnp.concatenate([high, low], axis=1), both_ref[index], preferred_element_type=F32
            ) + jnp.dot(high, low_ref[index], preferred_element_type=F32)
            row = pl.multiple_of(info_ref[index, 0] * BLK, BLK)
            for q in range(count):
                for odd in range(2):
                    spot = pl.ds(row + odd, ROWS, stride=2)
                    half[q, spot, :] += part[q * ROWS : (q + 1) * ROWS, odd * 128 : odd * 128 + 128]
    for q in range(count):
        high, low = split(half[q])
        high_ref[:, q * 128 : (q + 1) * 128] = high
        low_half_ref[:, q * 128 : (q + 1) * 128] = low

    def columns(ref, step):
        start = (lax.rem(y + step, NY) * NC + core) * 128
        return ref[pl.ds(pl.multiple_of(start, 128), 128), :]

    for pair in range(2):
        col_high = jnp.concatenate([columns(high_ref, 2 * pair + j) for j in range(2)], axis=0)
        col_low = jnp.concatenate([columns(low_half_ref, 2 * pair + j) for j in range(2)], axis=0)
        where = slice(pair * 256, pair * 256 + 256)
        value = lax.dot_general(high_ref[...], col_high, NT, preferred_element_type=F32)
        value += lax.dot_general(high_ref[...], col_low, NT, preferred_element_type=F32)
        value += lax.dot_general(low_half_ref[...], col_high, NT, preferred_element_type=F32)
        if not first:
            value += before[:, where]
        if last:
            total[:, where] = value
        else:
            outs[0][:, where] = value
    if last:
        for which in range(2):

            @pl.when(core == which)
            def _():
                for a in range(4):
                    for b in range(4):
                        i, j = (b, a) if which == 0 else (a, b)
                        start = pl.multiple_of(lax.rem(x + i, NX) * 256, 256)
                        outs[a][b] = total[pl.ds(start, 256), j * 128 : (j + 1) * 128]


def per_device(blocks, pair_list, pair_count, orbitals):
    aux, occ = lax.axis_index("aux"), lax.axis_index("occ")
    x, y, core = aux // NZ, occ // NC, occ % NC
    live = (2 * occ + jnp.arange(2) < pair_count[0]).astype(jnp.int32)
    own = jnp.concatenate([pair_list[0], live[:, None]], axis=1).reshape(6)
    info = jnp.concatenate([y[None], own]).astype(jnp.int32)
    place = jnp.stack([y, x, core]).astype(jnp.int32)
    tiles = blocks.reshape(AUX_DEV, 2, ROWS, 128)
    tiles = with_layout_constraint(tiles, Layout(major_to_minor=(0, 2, 1, 3)))
    tiles = tiles.transpose(0, 2, 1, 3).reshape(AUX_DEV * BLK, 128)

    def payload(chunk):
        return jax.ShapeDtypeStruct(
            (2 * CHUNKS[chunk] * ROWS + (HEAD if chunk == 0 else 0), 128), F32
        )

    packed = call(pack_kernel, [payload(c) for c in range(2) for _ in range(NY)], [SMEM, VMEM])(
        info, tiles
    )
    arrived = []
    for chunk in range(2):
        mine = packed[chunk * NY : chunk * NY + NY]
        got = [mine[0]] + [
            send(mine[k], lambda x, z, y, c, k=k: (x, z, y + k, c)) for k in (2, 1, 3)
        ]
        other = [send(part, lambda x, z, y, c: (x, z, y, c + 1)) for part in got]
        arrived.append(got + other)
    heads = jnp.stack([part[2 * CHUNKS[0] * ROWS, :6] for part in arrived[0]])
    pairs = heads.astype(jnp.int32).reshape(16, 3)
    both, low = call(
        weights_kernel,
        [jax.ShapeDtypeStruct((16, 256, 256), BF16), jax.ShapeDtypeStruct((16, 128, 256), BF16)],
        [SMEM, VMEM],
        [pltpu.VMEM((NBF, NOCC), BF16)] * 2,
    )(pairs, orbitals)
    total = None
    for chunk, count in enumerate(CHUNKS):
        first, last = chunk == 0, chunk == 1
        outs = (
            [jax.ShapeDtypeStruct((4, 256, 128), F32)] * 4
            if last
            else [jax.ShapeDtypeStruct((NBF, 512), F32)]
        )
        total = call(
            functools.partial(product_kernel, count, first, last),
            outs,
            [SMEM, SMEM] + [VMEM] * (10 if first else 11),
            [
                pltpu.VMEM((count, NBF, NOCC), F32),
                pltpu.VMEM((NBF, count * NOCC), BF16),
                pltpu.VMEM((NBF, count * NOCC), BF16),
                pltpu.VMEM((NBF, 512) if last else (8, 128), F32),
            ],
            flops=2 * 3 * NBF * 512 * count * NOCC,
        )(pairs, place, both, low, *arrived[chunk], *([] if first else total))

    def along(k, swapped):
        def where(x, z, y, c):
            return (x + k, z, y, c) if (c == 1) != swapped else (x, z, y + k, c)

        return where

    summed = total[0]
    got = [send(total[k], along(k, False)) for k in (2, 1, 3)]
    summed = total[0] + got[0] + got[1] + got[2]
    got = [send(summed[k], along(k, True)) for k in (2, 1, 3)]
    summed = summed[0] + got[0] + got[1] + got[2]
    groups = [[a * NZ + b for b in range(NZ)] for a in range(NX)]
    parts = lax.all_to_all(
        summed.reshape(NZ, 32, 128), "aux", 0, 0, axis_index_groups=groups, tiled=True
    )
    return jnp.sum(parts, axis=0)


def solution(mesh):
    in_specs = (P("aux", "occ", None), P("aux", "occ", None), P("aux"), P())
    return jax.shard_map(
        per_device, mesh=mesh, in_specs=in_specs, out_specs=P("aux", "occ"), check_vma=False
    )
```

time: 181 us -> 88.7 us (0.49)
  waiting for transfers between devices: 74.1 us -> 32.2 us
  matrix products: 29.5 us -> 0 us
  local copies, waits for them, and re-layouts: 22.9 us -> 2.67 us
  between operations: 14.1 us -> 0.77 us
  Pallas kernels: 0 us -> 13.1 us
  blocking collectives: 26.8 us -> 17.3 us
  starting transfers between devices: 10.2 us -> 19.7 us
    reduce_scatter x1 -> x0, waiting for transfers between devices: 38.4 us -> none  [per_device(): lax.psum_scatter(partial_value, 'occ', scatter_dimension=1, tiled=True)]
    all_to_all x2 -> x0, waiting for transfers between devices: 35.7 us -> none  [the longest x1 35.7 us: per_device(): lax.all_to_all(half_tiles.reshape(orbital_count, slot_count, aux_rows * B...]
    ppermute x0 -> x20, waiting for transfers between devices: none -> 32.2 us  [send(): return lax.ppermute(array, ('aux', 'occ'), pairs)]
    dot_general x4 -> x0, matrix products: 29.5 us -> none  [the longest x1 11.8 us: per_device(): jnp.einsum('isqm,sM->iqMm', owned_rows, row_onehot, precision=lax.Precisi...]
    ppermute x0 -> x20, starting transfers between devices: none -> 19.7 us  [send(): return lax.ppermute(array, ('aux', 'occ'), pairs)]
    reshape x4 -> x1, local copies, waits for them, and re-layouts: 17.4 us -> 0.08 us  [per_device(): own = jnp.concatenate([pair_list[0], live[:, None]], axis=1).reshape(6)]
    pallas_call x0 -> x4, Pallas kernels: none -> 13.1 us  [the longest x2 11.2 us: per_device(): call(functools.partial(product_kernel, count, first, last), outs, [SMEM,...]
    all_to_all x2 -> x0, starting transfers between devices: 10.2 us -> none  [the longest x1 5.4 us: copy_for_each(): lax.all_to_all(jnp.broadcast_to(array[None], (devices, *array.shape)), ax...]
  transfers between devices with their start and end apart: 3 -> 20, of which waited for: 2 -> 10; matrix products, arithmetic and copies ran while one was open for 10% -> 0% of each run, Pallas kernels for 0% -> 10%
where the time goes in v1:
time: 88.7 us; the launch traced here: 87.5 us
  waiting for transfers between devices  32.2 us (36%)
  starting transfers between devices  19.7 us (22%)
  blocking collectives  17.3 us (20%)
  Pallas kernels  13.1 us (15%)
  local copies, waits for them, and re-layouts  2.67 us (3%)
  other arithmetic  1.71 us (2%)
    ppermute x20, waiting for transfers between devices, send(): return lax.ppermute(array, ('aux', 'occ'), pairs)  32.2 us
    ppermute x20, starting transfers between devices, send(): return lax.ppermute(array, ('aux', 'occ'), pairs)  19.7 us
    all_to_all x1, blocking collectives, per_device(): lax.all_to_all(summed.reshape(NZ, 32, 128), 'aux', 0, 0, axis_index_group...  17.3 us
    pallas_call x2, Pallas kernels, per_device(): call(functools.partial(product_kernel, count, first, last), outs, [SMEM,...  11.2 us
    unnamed x4, local copies, waits for them, and re-layouts  2.45 us
  transfers between devices with their start and end apart: 20, of which 10 were waited for; matrix products, arithmetic and copies ran while one was open for 0% of the time, Pallas kernels for 10%

profile of v1, /device:TPU:8, one launch (start us, length us, event | category | flops | bytes accessed | tf_op | source)
XLA Modules:
  0.0 87.5 jit_solution(10516141336165154426)
XLA Ops:
  0.7 0.8 pad_add_fusion
  1.4 0.1 reshape.28
  1.5 0.1 pad_add_fusion.1.info_ref
  1.6 0.0 copy-start
  1.6 1.4 %copy-done = f32[48,2,4096]{2,1,0:T(2,128)S(1)} copy-done((f32[48,2,4096]{2,1,0:T(2,128)S(1)}, f32[48,2,4096]{2,1,0:T(2,128)}, u32[]{:S(2)}) %copy-start) | copy-done | bytes 1572888
  3.0 0.7 shard_map.46
  3.7 2.4 %collective-permute-start = (f32[520,128]{1,0:T(8,128)S(1)}, f32[520,128]{1,0:T(8,128)S(1)}, u32[]{:S(2)}, u32[]{:S(2)}) collective-permute-start(f32[520,128]{1,0:T(8,128)S(1)} %get-tuple-element.20), channel_id=1, source_target_pairs={{0,4},{1,5},{2,6},{3,7},{4,0},{5,1},{6,2},{7,3},{8,12},{9,13},{10,... | collective-permute-start | bytes 798728 | tf_op jit(solution)/shard_map/ppermute | solution.py:37
  6.0 1.4 %collective-permute-start.1 = (f32[520,128]{1,0:T(8,128)S(1)}, f32[520,128]{1,0:T(8,128)S(1)}, u32[]{:S(2)}, u32[]{:S(2)}) collective-permute-start(f32[520,128]{1,0:T(8,128)S(1)} %get-tuple-element.21), channel_id=1, source_target_pairs={{0,2},{1,3},{2,4},{3,5},{4,6},{5,7},{6,0},{7,1},{8,10},{9,11},{10,... | collective-permute-start | bytes 798728 | tf_op jit(solution)/shard_map/ppermute | solution.py:37
  7.4 0.7 collective-permute-start.2
  8.1 0.0 collective-permute-start.3
  8.1 6.5 %collective-permute-done.refs_1_ = f32[520,128]{1,0:T(8,128)S(1)} collective-permute-done((f32[520,128]{1,0:T(8,128)S(1)}, f32[520,128]{1,0:T(8,128)S(1)}, u32[]{:S(2)}, u32[]{:S(2)}) %collective-permute-start) | collective-permute-done | bytes 266272 | tf_op jit(solution)/shard_map/ppermute | solution.py:37
  14.6 0.0 collective-permute-start.4
  14.6 4.7 %collective-permute-done.1.refs_2_ = f32[520,128]{1,0:T(8,128)S(1)} collective-permute-done((f32[520,128]{1,0:T(8,128)S(1)}, f32[520,128]{1,0:T(8,128)S(1)}, u32[]{:S(2)}, u32[]{:S(2)}) %collective-permute-start.1) | collective-permute-done | bytes 266272 | tf_op jit(solution)/shard_map/ppermute | solution.py:37
  19.2 0.0 collective-permute-start.5
  19.3 0.0 collective-permute-done.2.refs_3_
  19.3 0.5 collective-permute-start.6
  19.8 1.6 %collective-permute-start.7 = (f32[256,128]{1,0:T(8,128)S(1)}, f32[256,128]{1,0:T(8,128)S(1)}, u32[]{:S(2)}, u32[]{:S(2)}) collective-permute-start(f32[256,128]{1,0:T(8,128)S(1)} %get-tuple-element.26), channel_id=1, source_target_pairs={{0,4},{1,5},{2,6},{3,7},{4,0},{5,1},{6,2},{7,3},{8,12},{9,13},{10,... | collective-permute-start | bytes 393224 | tf_op jit(solution)/shard_map/ppermute | solution.py:37
  21.4 0.0 collective-permute-done.3.refs_4_
  21.4 0.1 collective-permute-start.8
  21.5 0.0 collective-permute-done.4.refs_5_
  21.5 2.0 %collective-permute-start.9 = (f32[256,128]{1,0:T(8,128)S(1)}, f32[256,128]{1,0:T(8,128)S(1)}, u32[]{:S(2)}, u32[]{:S(2)}) collective-permute-start(f32[256,128]{1,0:T(8,128)S(1)} %get-tuple-element.28), channel_id=1, source_target_pairs={{0,6},{1,7},{2,0},{3,1},{4,2},{5,3},{6,4},{7,5},{8,14},{9,15},{10,... | collective-permute-start | bytes 393224 | tf_op jit(solution)/shard_map/ppermute | solution.py:37
  23.4 0.1 pad_add_fusion.2.place_ref
  23.5 4.1 %collective-permute-done.7.refs_1_ = f32[256,128]{1,0:T(8,128)S(1)} collective-permute-done((f32[256,128]{1,0:T(8,128)S(1)}, f32[256,128]{1,0:T(8,128)S(1)}, u32[]{:S(2)}, u32[]{:S(2)}) %collective-permute-start.7) | collective-permute-done | bytes 131104 | tf_op jit(solution)/shard_map/ppermute | solution.py:37
  27.6 0.0 collective-permute-start.10
  27.6 1.1 %collective-permute-done.8.refs_2_ = f32[256,128]{1,0:T(8,128)S(1)} collective-permute-done((f32[256,128]{1,0:T(8,128)S(1)}, f32[256,128]{1,0:T(8,128)S(1)}, u32[]{:S(2)}, u32[]{:S(2)}) %collective-permute-start.8) | collective-permute-done | bytes 131104 | tf_op jit(solution)/shard_map/ppermute | solution.py:37
  28.7 0.0 collective-permute-start.11
  28.7 0.8 collective-permute-done.9.refs_3_
  29.5 0.0 collective-permute-start.12
  29.5 0.0 collective-permute-done.5.refs_6_
  29.5 0.5 collective-permute-start.13
  30.0 0.0 collective-permute-done.6.refs_7_
  30.0 0.1 convert_element_type.19.info_ref
  30.1 0.0 copy-start.1
  30.1 1.0 %copy-done.1 = f32[128,1024]{1,0:T(8,128)S(1)} copy-done((f32[128,1024]{1,0:T(8,128)S(1)}, f32[128,1024]{1,0:T(8,128)}, u32[]{:S(2)}) %copy-start.1) | copy-done | bytes 524312
  31.2 1.3 %shard_map.47 = (bf16[16,256,256]{2,1,0:T(8,128)(2,1)S(1)}, bf16[16,128,256]{2,1,0:T(8,128)(2,1)S(1)}) custom-call(s32[16,3]{1,0:T(8,128)S(1)} %convert_element_type.19.info_ref, f32[128,1024]{1,0:T(8,128)S(1)} %copy-done.1), custom_call_target="tpu_custom_call" | custom-call | tf_op jit(solution)/shard_map/pallas_call | solution.py:188
  32.4 7.1 %shard_map.48.refs_8_ = f32[1024,512]{1,0:T(8,128)S(1)} custom-call(s32[16,3]{1,0:T(8,128)S(1)} %convert_element_type.19.info_ref, s32[3]{0:T(128)S(1)} %pad_add_fusion.2.place_ref, bf16[16,256,256]{2,1,0:T(8,128)(2,1)S(1)} %get-tuple-element.23.both_ref, bf16[16,128,256]{2,1,0:T(8,128)(2,1)S(1)} %get-tuple-element.24.low_ref, ...), custom_call_target="tpu_custom_call" | custom-call | flops 3221225472 | tf_op jit(solution)/shard_map/pallas_call | solution.py:202
  39.6 0.0 collective-permute-done.10.refs_4_
  39.6 0.0 collective-permute-done.11.refs_5_
  39.6 0.0 collective-permute-done.12.refs_6_
  39.6 0.0 collective-permute-done.13.refs_7_
  39.6 4.0 %shard_map.49 = (f32[4,256,128]{2,1,0:T(8,128)S(1)}, f32[4,256,128]{2,1,0:T(8,128)S(1)}, f32[4,256,128]{2,1,0:T(8,128)S(1)}, f32[4,256,128]{2,1,0:T(8,128)S(1)}) custom-call(s32[16,3]{1,0:T(8,128)S(1)} %convert_element_type.19.info_ref, s32[3]{0:T(128)S(1)} %pad_add_fusion.2.place_ref, bf16[16,256,256]{2,1,0:T(8,128)(2,1)S(1)} %get-tuple-element.23.both_ref, ...), custom_call_target="tpu_custom_call" | custom-call | flops 1610612736 | tf_op jit(solution)/shard_map/pallas_call | solution.py:202
  43.7 2.2 %collective-permute-start.14 = (f32[4,256,128]{2,1,0:T(8,128)S(1)}, f32[4,256,128]{2,1,0:T(8,128)S(1)}, u32[]{:S(2)}, u32[]{:S(2)}) collective-permute-start(f32[4,256,128]{2,1,0:T(8,128)S(1)} %get-tuple-element.30), channel_id=1, source_target_pairs={{0,4},{1,129},{2,6},{3,131},{4,0},{5,133},{6,2},{7,135},{8,12},{9,... | collective-permute-start | bytes 1572872 | tf_op jit(solution)/shard_map/ppermute | solution.py:37
  45.9 0.3 collective-permute-start.15
  46.2 1.7 %collective-permute-start.16 = (f32[4,256,128]{2,1,0:T(8,128)S(1)}, f32[4,256,128]{2,1,0:T(8,128)S(1)}, u32[]{:S(2)}, u32[]{:S(2)}) collective-permute-start(f32[4,256,128]{2,1,0:T(8,128)S(1)} %get-tuple-element.32), channel_id=1, source_target_pairs={{0,6},{1,193},{2,0},{3,195},{4,2},{5,197},{6,4},{7,199},{8,14},{9,... | collective-permute-start | bytes 1572872 | tf_op jit(solution)/shard_map/ppermute | solution.py:37
  47.9 6.7 %collective-permute-done.14 = f32[4,256,128]{2,1,0:T(8,128)S(1)} collective-permute-done((f32[4,256,128]{2,1,0:T(8,128)S(1)}, f32[4,256,128]{2,1,0:T(8,128)S(1)}, u32[]{:S(2)}, u32[]{:S(2)}) %collective-permute-start.14) | collective-permute-done | bytes 524320 | tf_op jit(solution)/shard_map/ppermute | solution.py:37
  54.5 5.0 %collective-permute-done.15 = f32[4,256,128]{2,1,0:T(8,128)S(1)} collective-permute-done((f32[4,256,128]{2,1,0:T(8,128)S(1)}, f32[4,256,128]{2,1,0:T(8,128)S(1)}, u32[]{:S(2)}, u32[]{:S(2)}) %collective-permute-start.15) | collective-permute-done | bytes 524320 | tf_op jit(solution)/shard_map/ppermute | solution.py:37
  59.5 0.5 collective-permute-done.16
  60.1 0.1 add_add_fusion
  60.2 3.1 %collective-permute-start.17 = (f32[256,128]{1,0:T(8,128)S(1)}, f32[256,128]{1,0:T(8,128)S(1)}, u32[]{:S(2)}, u32[]{:S(2)}) collective-permute-start(f32[256,128]{1,0:T(8,128)S(1)} %get-tuple-element.33), channel_id=1, source_target_pairs={{0,128},{1,5},{2,130},{3,7},{4,132},{5,1},{6,134},{7,3},{8,136},{9... | collective-permute-start | bytes 393224 | tf_op jit(solution)/shard_map/ppermute | solution.py:37
  63.3 0.6 collective-permute-start.18
  63.9 2.6 %collective-permute-start.19 = (f32[256,128]{1,0:T(8,128)S(1)}, f32[256,128]{1,0:T(8,128)S(1)}, u32[]{:S(2)}, u32[]{:S(2)}) collective-permute-start(f32[256,128]{1,0:T(8,128)S(1)} %get-tuple-element.34), channel_id=1, source_target_pairs={{0,192},{1,7},{2,194},{3,1},{4,196},{5,3},{6,198},{7,5},{8,200},{9... | collective-permute-start | bytes 393224 | tf_op jit(solution)/shard_map/ppermute | solution.py:37
  66.6 0.2 collective-permute-done.17
  66.8 2.7 %collective-permute-done.18 = f32[256,128]{1,0:T(8,128)S(1)} collective-permute-done((f32[256,128]{1,0:T(8,128)S(1)}, f32[256,128]{1,0:T(8,128)S(1)}, u32[]{:S(2)}, u32[]{:S(2)}) %collective-permute-start.18) | collective-permute-done | bytes 131104 | tf_op jit(solution)/shard_map/ppermute | solution.py:37
  69.5 0.0 collective-permute-done.19
  69.6 17.3 %all_to_all.5 = f32[8,32,128]{2,1,0:T(8,128)S(1)} all-to-all(f32[8,32,128]{2,1,0:T(8,128)S(1)} %bitcast.27), channel_id=1, replica_groups={{0,8,16,24,32,40,48,56},{64,72,80,88,96,104,112,120},{128,136,144,152,1..., dimensions={0} | all-to-all | bytes 262144 | tf_op jit(solution)/shard_map/all_to_all | solution.py:227
  86.9 0.6 reduce_sum.9
  (13 shorter events, 0.1 us)
Async XLA Ops:
  1.6 1.4 %copy-start = (f32[48,2,4096]{2,1,0:T(2,128)S(1)}, f32[48,2,4096]{2,1,0:T(2,128)}, u32[]{:S(2)}) copy-start(f32[48,2,4096]{2,1,0:T(2,128)} %param.4) | copy-start | bytes 4718596
  3.7 10.9 %collective-permute-start = (f32[520,128]{1,0:T(8,128)S(1)}, f32[520,128]{1,0:T(8,128)S(1)}, u32[]{:S(2)}, u32[]{:S(2)}) collective-permute-start(f32[520,128]{1,0:T(8,128)S(1)} %get-tuple-element.20), channel_id=1, source_target_pairs={{0,4},{1,5},{2,6},{3,7},{4,0},{5,1},{6,2},{7,3},{8,12},{9,13},{10,... | collective-permute-start | bytes 798728 | tf_op jit(solution)/shard_map/ppermute | solution.py:37
  6.0 13.2 %collective-permute-start.1 = (f32[520,128]{1,0:T(8,128)S(1)}, f32[520,128]{1,0:T(8,128)S(1)}, u32[]{:S(2)}, u32[]{:S(2)}) collective-permute-start(f32[520,128]{1,0:T(8,128)S(1)} %get-tuple-element.21), channel_id=1, source_target_pairs={{0,2},{1,3},{2,4},{3,5},{4,6},{5,7},{6,0},{7,1},{8,10},{9,11},{10,... | collective-permute-start | bytes 798728 | tf_op jit(solution)/shard_map/ppermute | solution.py:37
  7.4 11.9 %collective-permute-start.2 = (f32[520,128]{1,0:T(8,128)S(1)}, f32[520,128]{1,0:T(8,128)S(1)}, u32[]{:S(2)}, u32[]{:S(2)}) collective-permute-start(f32[520,128]{1,0:T(8,128)S(1)} %get-tuple-element.22), channel_id=1, source_target_pairs={{0,6},{1,7},{2,0},{3,1},{4,2},{5,3},{6,4},{7,5},{8,14},{9,15},{10,... | collective-permute-start | bytes 798728 | tf_op jit(solution)/shard_map/ppermute | solution.py:37
  8.1 13.3 %collective-permute-start.3 = (f32[520,128]{1,0:T(8,128)S(1)}, f32[520,128]{1,0:T(8,128)S(1)}, u32[]{:S(2)}, u32[]{:S(2)}) collective-permute-start(f32[520,128]{1,0:T(8,128)S(1)} %get-tuple-element.19.refs_0_), channel_id=1, source_target_pairs={{0,1},{1,0},{2,3},{3,2},{4,5},{5,4},{6,7},{7,6},{8,9},{9,8},{10,11... | collective-permute-start | bytes 798728 | tf_op jit(solution)/shard_map/ppermute | solution.py:37
  14.6 6.9 %collective-permute-start.4 = (f32[520,128]{1,0:T(8,128)S(1)}, f32[520,128]{1,0:T(8,128)S(1)}, u32[]{:S(2)}, u32[]{:S(2)}) collective-permute-start(f32[520,128]{1,0:T(8,128)S(1)} %collective-permute-done.refs_1_), channel_id=1, source_target_pairs={{0,1},{1,0},{2,3},{3,2},{4,5},{5,4},{6,7},{7,6},{8,9},{9,8},{10,11... | collective-permute-start | bytes 798728 | tf_op jit(solution)/shard_map/ppermute | solution.py:37
  19.2 10.3 %collective-permute-start.5 = (f32[520,128]{1,0:T(8,128)S(1)}, f32[520,128]{1,0:T(8,128)S(1)}, u32[]{:S(2)}, u32[]{:S(2)}) collective-permute-start(f32[520,128]{1,0:T(8,128)S(1)} %collective-permute-done.1.refs_2_), channel_id=1, source_target_pairs={{0,1},{1,0},{2,3},{3,2},{4,5},{5,4},{6,7},{7,6},{8,9},{9,8},{10,11... | collective-permute-start | bytes 798728 | tf_op jit(solution)/shard_map/ppermute | solution.py:37
  19.3 10.7 %collective-permute-start.6 = (f32[520,128]{1,0:T(8,128)S(1)}, f32[520,128]{1,0:T(8,128)S(1)}, u32[]{:S(2)}, u32[]{:S(2)}) collective-permute-start(f32[520,128]{1,0:T(8,128)S(1)} %collective-permute-done.2.refs_3_), channel_id=1, source_target_pairs={{0,1},{1,0},{2,3},{3,2},{4,5},{5,4},{6,7},{7,6},{8,9},{9,8},{10,11... | collective-permute-start | bytes 798728 | tf_op jit(solution)/shard_map/ppermute | solution.py:37
  19.8 7.9 %collective-permute-start.7 = (f32[256,128]{1,0:T(8,128)S(1)}, f32[256,128]{1,0:T(8,128)S(1)}, u32[]{:S(2)}, u32[]{:S(2)}) collective-permute-start(f32[256,128]{1,0:T(8,128)S(1)} %get-tuple-element.26), channel_id=1, source_target_pairs={{0,4},{1,5},{2,6},{3,7},{4,0},{5,1},{6,2},{7,3},{8,12},{9,13},{10,... | collective-permute-start | bytes 393224 | tf_op jit(solution)/shard_map/ppermute | solution.py:37
  21.4 7.3 %collective-permute-start.8 = (f32[256,128]{1,0:T(8,128)S(1)}, f32[256,128]{1,0:T(8,128)S(1)}, u32[]{:S(2)}, u32[]{:S(2)}) collective-permute-start(f32[256,128]{1,0:T(8,128)S(1)} %get-tuple-element.27), channel_id=1, source_target_pairs={{0,2},{1,3},{2,4},{3,5},{4,6},{5,7},{6,0},{7,1},{8,10},{9,11},{10,... | collective-permute-start | bytes 393224 | tf_op jit(solution)/shard_map/ppermute | solution.py:37
  21.5 8.0 %collective-permute-start.9 = (f32[256,128]{1,0:T(8,128)S(1)}, f32[256,128]{1,0:T(8,128)S(1)}, u32[]{:S(2)}, u32[]{:S(2)}) collective-permute-start(f32[256,128]{1,0:T(8,128)S(1)} %get-tuple-element.28), channel_id=1, source_target_pairs={{0,6},{1,7},{2,0},{3,1},{4,2},{5,3},{6,4},{7,5},{8,14},{9,15},{10,... | collective-permute-start | bytes 393224 | tf_op jit(solution)/shard_map/ppermute | solution.py:37
  27.6 11.9 %collective-permute-start.10 = (f32[256,128]{1,0:T(8,128)S(1)}, f32[256,128]{1,0:T(8,128)S(1)}, u32[]{:S(2)}, u32[]{:S(2)}) collective-permute-start(f32[256,128]{1,0:T(8,128)S(1)} %get-tuple-element.25.refs_0_), channel_id=1, source_target_pairs={{0,1},{1,0},{2,3},{3,2},{4,5},{5,4},{6,7},{7,6},{8,9},{9,8},{10,11... | collective-permute-start | bytes 393224 | tf_op jit(solution)/shard_map/ppermute | solution.py:37
  28.7 10.9 %collective-permute-start.11 = (f32[256,128]{1,0:T(8,128)S(1)}, f32[256,128]{1,0:T(8,128)S(1)}, u32[]{:S(2)}, u32[]{:S(2)}) collective-permute-start(f32[256,128]{1,0:T(8,128)S(1)} %collective-permute-done.7.refs_1_), channel_id=1, source_target_pairs={{0,1},{1,0},{2,3},{3,2},{4,5},{5,4},{6,7},{7,6},{8,9},{9,8},{10,11... | collective-permute-start | bytes 393224 | tf_op jit(solution)/shard_map/ppermute | solution.py:37
  29.5 10.1 %collective-permute-start.12 = (f32[256,128]{1,0:T(8,128)S(1)}, f32[256,128]{1,0:T(8,128)S(1)}, u32[]{:S(2)}, u32[]{:S(2)}) collective-permute-start(f32[256,128]{1,0:T(8,128)S(1)} %collective-permute-done.8.refs_2_), channel_id=1, source_target_pairs={{0,1},{1,0},{2,3},{3,2},{4,5},{5,4},{6,7},{7,6},{8,9},{9,8},{10,11... | collective-permute-start | bytes 393224 | tf_op jit(solution)/shard_map/ppermute | solution.py:37
  29.5 10.1 %collective-permute-start.13 = (f32[256,128]{1,0:T(8,128)S(1)}, f32[256,128]{1,0:T(8,128)S(1)}, u32[]{:S(2)}, u32[]{:S(2)}) collective-permute-start(f32[256,128]{1,0:T(8,128)S(1)} %collective-permute-done.9.refs_3_), channel_id=1, source_target_pairs={{0,1},{1,0},{2,3},{3,2},{4,5},{5,4},{6,7},{7,6},{8,9},{9,8},{10,11... | collective-permute-start | bytes 393224 | tf_op jit(solution)/shard_map/ppermute | solution.py:37
  30.1 1.0 %copy-start.1 = (f32[128,1024]{1,0:T(8,128)S(1)}, f32[128,1024]{1,0:T(8,128)}, u32[]{:S(2)}) copy-start(f32[128,1024]{1,0:T(8,128)} %orbitals_ref.1) | copy-start | bytes 1572868
  43.7 10.9 %collective-permute-start.14 = (f32[4,256,128]{2,1,0:T(8,128)S(1)}, f32[4,256,128]{2,1,0:T(8,128)S(1)}, u32[]{:S(2)}, u32[]{:S(2)}) collective-permute-start(f32[4,256,128]{2,1,0:T(8,128)S(1)} %get-tuple-element.30), channel_id=1, source_target_pairs={{0,4},{1,129},{2,6},{3,131},{4,0},{5,133},{6,2},{7,135},{8,12},{9,... | collective-permute-start | bytes 1572872 | tf_op jit(solution)/shard_map/ppermute | solution.py:37
  45.9 13.7 %collective-permute-start.15 = (f32[4,256,128]{2,1,0:T(8,128)S(1)}, f32[4,256,128]{2,1,0:T(8,128)S(1)}, u32[]{:S(2)}, u32[]{:S(2)}) collective-permute-start(f32[4,256,128]{2,1,0:T(8,128)S(1)} %get-tuple-element.31), channel_id=1, source_target_pairs={{0,2},{1,65},{2,4},{3,67},{4,6},{5,69},{6,0},{7,71},{8,10},{9,73},... | collective-permute-start | bytes 1572872 | tf_op jit(solution)/shard_map/ppermute | solution.py:37
  46.2 13.9 %collective-permute-start.16 = (f32[4,256,128]{2,1,0:T(8,128)S(1)}, f32[4,256,128]{2,1,0:T(8,128)S(1)}, u32[]{:S(2)}, u32[]{:S(2)}) collective-permute-start(f32[4,256,128]{2,1,0:T(8,128)S(1)} %get-tuple-element.32), channel_id=1, source_target_pairs={{0,6},{1,193},{2,0},{3,195},{4,2},{5,197},{6,4},{7,199},{8,14},{9,... | collective-permute-start | bytes 1572872 | tf_op jit(solution)/shard_map/ppermute | solution.py:37
  60.2 6.6 %collective-permute-start.17 = (f32[256,128]{1,0:T(8,128)S(1)}, f32[256,128]{1,0:T(8,128)S(1)}, u32[]{:S(2)}, u32[]{:S(2)}) collective-permute-start(f32[256,128]{1,0:T(8,128)S(1)} %get-tuple-element.33), channel_id=1, source_target_pairs={{0,128},{1,5},{2,130},{3,7},{4,132},{5,1},{6,134},{7,3},{8,136},{9... | collective-permute-start | bytes 393224 | tf_op jit(solution)/shard_map/ppermute | solution.py:37
  63.3 6.2 %collective-permute-start.18 = (f32[256,128]{1,0:T(8,128)S(1)}, f32[256,128]{1,0:T(8,128)S(1)}, u32[]{:S(2)}, u32[]{:S(2)}) collective-permute-start(f32[256,128]{1,0:T(8,128)S(1)} %get-tuple-element.35), channel_id=1, source_target_pairs={{0,64},{1,3},{2,66},{3,5},{4,68},{5,7},{6,70},{7,1},{8,72},{9,11},... | collective-permute-start | bytes 393224 | tf_op jit(solution)/shard_map/ppermute | solution.py:37
  63.9 5.6 %collective-permute-start.19 = (f32[256,128]{1,0:T(8,128)S(1)}, f32[256,128]{1,0:T(8,128)S(1)}, u32[]{:S(2)}, u32[]{:S(2)}) collective-permute-start(f32[256,128]{1,0:T(8,128)S(1)} %get-tuple-element.34), channel_id=1, source_target_pairs={{0,192},{1,7},{2,194},{3,1},{4,196},{5,3},{6,198},{7,5},{8,200},{9... | collective-permute-start | bytes 393224 | tf_op jit(solution)/shard_map/ppermute | solution.py:37

commit v2 on v0

v2 whole, which is shorter than its diff:
```python
import functools

import jax
import jax.numpy as jnp
from jax import lax
from jax.experimental import pallas as pl
from jax.experimental.layout import Layout, with_layout_constraint
from jax.experimental.pallas import tpu as pltpu
from jax.sharding import PartitionSpec as P

NBF = 1024
BLK = 64
NOCC = 128
AUX_DEV = 48
NX, NZ, NY, NC = 4, 8, 4, 2
CHIP_AUX = AUX_DEV // NY
CHUNKS = (8, 4)
STEPS = (2, 1, 3)
ROWS = BLK // 2
HEAD = 8
ORDER = 10**11
PAD = 8
VMEM = pl.BlockSpec(memory_space=pltpu.VMEM)
SMEM = pl.BlockSpec(memory_space=pltpu.SMEM)
F32, BF16 = jnp.float32, jnp.bfloat16
NT = (((1,), (1,)), ((), ()))


def device_of(x, z, y, c):
    return ((x % NX) * NZ + z % NZ) * (NY * NC) + (y % NY) * NC + c % NC


def send(array, where):
    pairs = [
        (device_of(x, z, y, c), device_of(*where(x, z, y, c)))
        for x in range(NX)
        for z in range(NZ)
        for y in range(NY)
        for c in range(NC)
    ]
    return lax.ppermute(array, ("aux", "occ"), pairs)


def call(kernel, out_shape, in_specs, scratch=(), flops=0, bytes_accessed=0):
    return pl.pallas_call(
        kernel,
        out_shape=out_shape,
        in_specs=in_specs,
        out_specs=jax.tree.map(lambda _: VMEM, out_shape),
        scratch_shapes=list(scratch),
        compiler_params=pltpu.CompilerParams(vmem_limit_bytes=40 * 2**20),
        cost_estimate=pl.CostEstimate(
            flops=flops, bytes_accessed=bytes_accessed, transcendentals=0
        ),
    )


def split(values):
    high = values.astype(BF16)
    return high, (values - high.astype(F32)).astype(BF16)


def pack_kernel(pairs_ref, count_ref, tiles_ref, own, *outs):
    occ = lax.axis_index("occ")
    lane = lax.broadcasted_iota(jnp.int32, (HEAD, 128), 1)
    head = jnp.zeros((HEAD, 128), F32)
    for slot in range(2):
        live = (occ * 2 + slot < count_ref[0]).astype(jnp.int32)
        for j, number in enumerate((pairs_ref[0, slot, 0], pairs_ref[0, slot, 1], live)):
            head = jnp.where(lane == 3 * slot + j, number.astype(F32), head)

    def fill(out, step, start, count, headed):
        chip = lax.rem(occ // NC + step, NY)
        base = (chip * CHIP_AUX + start) * BLK
        for slot in range(2):
            out[pl.ds(slot * count * ROWS, count * ROWS), :] = tiles_ref[
                pl.ds(pl.multiple_of(base, 8) + slot, count * ROWS, stride=2), :
            ]
        if headed:
            out[pl.ds(2 * count * ROWS, HEAD), :] = head

    fill(own, 0, 0, CHIP_AUX, True)
    for j, step in enumerate(STEPS):
        fill(outs[j], step, 0, CHUNKS[0], True)
        fill(outs[3 + j], step, CHUNKS[0], CHUNKS[1], False)


def orbitals_kernel(orbitals_ref, high_ref, low_ref):
    high, low = split(orbitals_ref[...].T)
    high_ref[...] = high
    low_ref[...] = low


def picked(ref, info_ref, index):
    column = pl.multiple_of(info_ref[index, 1] * BLK, BLK)
    block = ref[pl.ds(column, BLK), :].astype(F32)
    block = jnp.where(info_ref[index, 2] > 0, block, 0.0).astype(BF16)
    zero = jnp.zeros((BLK, NOCC), BF16)
    top = jnp.concatenate([block, zero], axis=1)
    return jnp.concatenate([top, jnp.concatenate([zero, block], axis=1)], axis=0)


def half_kernel(chunk, info_ref, high_t, low_t, own, own_other, *refs):
    got, (got_other, high_ref, low_ref, half, parts) = refs[:3], refs[3:]
    count, head = CHUNKS[chunk], HEAD if chunk == 0 else 0
    sources = [(ref, CHIP_AUX * ROWS, chunk * CHUNKS[0] * ROWS) for ref in (own, own_other)]
    sources += [(ref, count * ROWS, 0) for ref in got]
    sources += [(got_other, count * ROWS, j * (2 * count * ROWS + head)) for j in range(3)]
    half[...] = jnp.zeros_like(half)
    for source, (ref, stride, start) in enumerate(sources):
        for slot in range(2):
            index = source * 2 + slot
            high, low = split(ref[pl.ds(start + slot * stride, count * ROWS), :])
            weights = picked(high_t, info_ref, index)
            parts[index] = jnp.dot(
                jnp.concatenate([high, low], axis=1),
                jnp.concatenate([weights, weights], axis=0),
                preferred_element_type=F32,
            ) + jnp.dot(high, picked(low_t, info_ref, index), preferred_element_type=F32)
    for index in range(16):
        row = pl.multiple_of(info_ref[index, 0] * BLK, BLK)
        for q in range(count):
            for odd in range(2):
                spot = pl.ds(row + odd, ROWS, stride=2)
                half[q, spot, :] += parts[
                    index, q * ROWS : (q + 1) * ROWS, odd * 128 : odd * 128 + 128
                ]
    for q in range(count):
        high, low = split(half[q])
        high_ref[:, q * 128 : (q + 1) * 128] = high
        low_ref[:, q * 128 : (q + 1) * 128] = low


def exchange_kernel(steps, *refs):
    halves, outs = refs[:4], refs[4:]
    aux, occ = lax.axis_index("aux"), lax.axis_index("occ")
    x, y, core = aux // NZ, occ // NC, lax.rem(occ, NC)

    def rows(ref, i):
        return ref[pl.ds(pl.multiple_of(lax.rem(x + i, NX) * 256, 256), 256), :]

    def columns(ref, j):
        start = (lax.rem(y + j, NY) * NC + core) * 128
        return ref[pl.ds(pl.multiple_of(start, 128), 128), :]

    def product(row_steps, column_steps):
        value = None
        for part in range(2):
            high_ref, low_ref = halves[2 * part], halves[2 * part + 1]
            high, low = (
                jnp.concatenate([rows(ref, i) for i in row_steps], axis=0)
                for ref in (high_ref, low_ref)
            )
            col_high, col_low = (
                jnp.concatenate([columns(ref, j) for j in column_steps], axis=0)
                for ref in (high_ref, low_ref)
            )
            for left, right in ((high, col_high), (high, col_low), (low, col_high)):
                term = lax.dot_general(left, right, NT, preferred_element_type=F32)
                value = term if value is None else value + term
        return value

    @pl.when(core == 0)
    def _():
        value = product(range(NX), steps)
        for a in range(2):
            for b in range(4):
                outs[a][b * 256 : (b + 1) * 256] = value[b * 256 : (b + 1) * 256, a * 128 : (a + 1) * 128]

    @pl.when(core == 1)
    def _():
        for pair in range(2):
            value = product(steps, (2 * pair, 2 * pair + 1))
            for a in range(2):
                for b in range(2):
                    outs[a][(2 * pair + b) * 256 : (2 * pair + b + 1) * 256] = value[
                        a * 256 : (a + 1) * 256, b * 128 : (b + 1) * 128
                    ]
    for out in outs:
        if out.shape[0] > 1024:
            out[1024:] = jnp.zeros((out.shape[0] - 1024, 128), F32)


def per_device(blocks, pair_list, pair_count, orbitals):
    shape = jax.ShapeDtypeStruct
    tiles = blocks.reshape(AUX_DEV, 2, ROWS, 128)
    tiles = with_layout_constraint(tiles, Layout(major_to_minor=(0, 2, 1, 3)))
    tiles = tiles.transpose(0, 2, 1, 3).reshape(AUX_DEV * BLK, 128)
    first, second = CHUNKS
    own, *packed = call(
        pack_kernel,
        [shape((2 * CHIP_AUX * ROWS + HEAD, 128), F32)]
        + [shape((2 * first * ROWS + HEAD, 128), F32)] * 3
        + [shape((2 * second * ROWS, 128), F32)] * 3,
        [SMEM, SMEM, VMEM],
    )(pair_list, pair_count, tiles)
    high_t, low_t = call(orbitals_kernel, [shape((NBF, NOCC), BF16)] * 2, [VMEM], flops=ORDER)(orbitals)

    def over_y(mine):
        return [
            send(part, lambda x, z, y, c, k=k: (x, z, y + k, c))
            for part, k in zip(mine, STEPS, strict=True)
        ]

    def over_core(part):
        return send(part, lambda x, z, y, c: (x, z, y, c + 1))

    later = over_y(packed[3:])
    got = over_y(packed[:3])
    own_other = over_core(own)
    got_other = over_core(jnp.concatenate(got))
    size = 2 * first * ROWS + HEAD
    heads = [own[2 * CHIP_AUX * ROWS], own_other[2 * CHIP_AUX * ROWS]]
    heads += [part[size - HEAD] for part in got]
    heads += [got_other[(j + 1) * size - HEAD] for j in range(3)]
    pairs = jnp.stack(heads)[:, :6].astype(jnp.int32).reshape(16, 3)

    def half(chunk, *parts):
        count = CHUNKS[chunk]
        return call(
            functools.partial(half_kernel, chunk),
            [shape((NBF, count * NOCC), BF16)] * 2,
            [SMEM] + [VMEM] * 8,
            [pltpu.VMEM((count, NBF, NOCC), F32), pltpu.VMEM((16, count * ROWS, 256), F32)],
        )(pairs, high_t, low_t, own, own_other, *parts)

    halves = list(half(0, *got, got_other))
    halves[0], *later = lax.optimization_barrier((halves[0], *later))
    halves += half(1, *later, over_core(jnp.concatenate(later)))

    def along(k, swapped):
        def where(x, z, y, c):
            return (x + k, z, y, c) if (c == 1) != swapped else (x, z, y + k, c)

        return where

    def partial(steps):
        return call(
            functools.partial(exchange_kernel, steps),
            [shape((4 * 256 + (0 if 0 in steps else PAD), 128), F32)] * 2,
            [VMEM] * 4,
            flops=2 * 3 * 256 * 1024 * CHIP_AUX * NOCC,
        )(*halves)

    two, one = partial((2, 1))
    three, summed = partial((3, 0))
    for part, k in ((two, 2), (one, 1), (three, 3)):
        summed += send(part, along(k, False))[:1024]
    summed = summed.reshape(4, 256, 128)
    got = [send(summed[k], along(k, True)) for k in STEPS]
    summed = summed[0] + got[0] + got[1] + got[2]
    groups = [[a * NZ + b for b in range(NZ)] for a in range(NX)]
    parts = lax.all_to_all(
        summed.reshape(NZ, 32, 128), "aux", 0, 0, axis_index_groups=groups, tiled=True
    )
    return jnp.sum(parts, axis=0)


def solution(mesh):
    in_specs = (P("aux", "occ", None), P("aux", "occ", None), P("aux"), P())
    return jax.shard_map(
        per_device, mesh=mesh, in_specs=in_specs, out_specs=P("aux", "occ"), check_vma=False
    )
```

time: 181 us -> 80.2 us (0.44); the launches traced: 179 us -> 80 us
  waiting for transfers between devices: 74.1 us -> 25 us
  matrix products: 29.5 us -> 0 us
  local copies, waits for them, and re-layouts: 22.9 us -> 2.22 us
  Pallas kernels: 0 us -> 13.4 us
  between operations: 14.1 us -> 0.8 us
  starting transfers between devices: 10.2 us -> 20.3 us
  blocking collectives: 26.8 us -> 17.3 us
    reduce_scatter x1 -> x0, waiting for transfers between devices: 38.4 us -> none  [per_device(): lax.psum_scatter(partial_value, 'occ', scatter_dimension=1, tiled=True)]
    all_to_all x2 -> x0, waiting for transfers between devices: 35.7 us -> none  [the longest x1 35.7 us: per_device(): lax.all_to_all(half_tiles.reshape(orbital_count, slot_count, aux_rows * B...]
    dot_general x4 -> x0, matrix products: 29.5 us -> none  [the longest x1 11.8 us: per_device(): jnp.einsum('isqm,sM->iqMm', owned_rows, row_onehot, precision=lax.Precisi...]
    ppermute x0 -> x15, waiting for transfers between devices: none -> 25 us  [send(): return lax.ppermute(array, ('aux', 'occ'), pairs)]
    ppermute x0 -> x15, starting transfers between devices: none -> 20.3 us  [send(): return lax.ppermute(array, ('aux', 'occ'), pairs)]
    reshape x4 -> x1, local copies, waits for them, and re-layouts: 17.4 us -> 0.07 us  [per_device(): pairs = jnp.stack(heads)[:, :6].astype(jnp.int32).reshape(16, 3)]
    pallas_call x0 -> x6, Pallas kernels: none -> 13.4 us  [the longest x2 6.31 us: half(): call(functools.partial(half_kernel, chunk), [shape((NBF, count * NOCC), B...]
    all_to_all x2 -> x0, starting transfers between devices: 10.2 us -> none  [the longest x1 5.4 us: copy_for_each(): lax.all_to_all(jnp.broadcast_to(array[None], (devices, *array.shape)), ax...]
  transfers between devices with their start and end apart: 3 -> 15, of which waited for: 2 -> 10; matrix products, arithmetic and copies ran while one was open for 10% -> 0% of each run, Pallas kernels for 0% -> 9%
where the time goes in v2:
time: 80.2 us; the launch traced here: 80 us
  waiting for transfers between devices  25 us (31%)
  starting transfers between devices  20.3 us (25%)
  blocking collectives  17.3 us (22%)
  Pallas kernels  13.4 us (17%)
  local copies, waits for them, and re-layouts  2.22 us (3%)
  other arithmetic  0.93 us (1%)
    ppermute x15, waiting for transfers between devices, send(): return lax.ppermute(array, ('aux', 'occ'), pairs)  25 us
    ppermute x15, starting transfers between devices, send(): return lax.ppermute(array, ('aux', 'occ'), pairs)  20.3 us
    all_to_all x1, blocking collectives, per_device(): lax.all_to_all(summed.reshape(NZ, 32, 128), 'aux', 0, 0, axis_index_group...  17.3 us
    pallas_call x2, Pallas kernels, half(): call(functools.partial(half_kernel, chunk), [shape((NBF, count * NOCC), B...  6.31 us
    pallas_call x2, Pallas kernels, partial(): call(functools.partial(exchange_kernel, steps), [shape((4 * 256 + (0 if 0...  5.51 us
    unnamed x6, local copies, waits for them, and re-layouts  2.08 us
  transfers between devices with their start and end apart: 15, of which 10 were waited for; matrix products, arithmetic and copies ran while one was open for 0% of the time, Pallas kernels for 9%

profile of v2, /device:TPU:8, one launch (start us, length us, event | category | flops | bytes accessed | tf_op | source)
XLA Modules:
  0.0 80.0 jit_solution(18439201093018160096)
XLA Ops:
  0.7 0.0 copy-start
  0.7 1.4 %copy-done = f32[48,2,4096]{2,1,0:T(2,128)S(1)} copy-done((f32[48,2,4096]{2,1,0:T(2,128)S(1)}, f32[48,2,4096]{2,1,0:T(2,128)}, u32[]{:S(2)}) %copy-start) | copy-done | bytes 1572888
  2.1 0.0 copy-start.1
  2.1 0.7 copy-done.1
  2.7 0.0 copy-start.2
  2.7 1.3 %shard_map.46 = (f32[776,128]{1,0:T(8,128)S(1)}, f32[520,128]{1,0:T(8,128)S(1)}, f32[520,128]{1,0:T(8,128)S(1)}, f32[520,128]{1,0:T(8,128)S(1)}, f32[256,128]{1,...) custom-call(s32[1,2,2]{2,1,0:T(2,128)S(1)} %copy-done.1, s32[1]{0:T(128)S(6)} %copy.5.count_ref, ...), custom_call_target="tpu_custom_call" | custom-call | tf_op jit(solution)/shard_map/pallas_call | solution.py:190
  4.1 2.3 %collective-permute-start.1 = (f32[520,128]{1,0:T(8,128)S(1)}, f32[520,128]{1,0:T(8,128)S(1)}, u32[]{:S(2)}, u32[]{:S(2)}) collective-permute-start(f32[520,128]{1,0:T(8,128)S(1)} %get-tuple-element.27), channel_id=1, source_target_pairs={{0,4},{1,5},{2,6},{3,7},{4,0},{5,1},{6,2},{7,3},{8,12},{9,13},{10,... | collective-permute-start | bytes 798728 | tf_op jit(solution)/shard_map/ppermute | solution.py:41
  6.4 1.4 %collective-permute-start.2 = (f32[520,128]{1,0:T(8,128)S(1)}, f32[520,128]{1,0:T(8,128)S(1)}, u32[]{:S(2)}, u32[]{:S(2)}) collective-permute-start(f32[520,128]{1,0:T(8,128)S(1)} %get-tuple-element.28), channel_id=1, source_target_pairs={{0,2},{1,3},{2,4},{3,5},{4,6},{5,7},{6,0},{7,1},{8,10},{9,11},{10,... | collective-permute-start | bytes 798728 | tf_op jit(solution)/shard_map/ppermute | solution.py:41
  7.7 0.7 collective-permute-start.3
  8.4 1.4 %collective-permute-start.5 = (f32[256,128]{1,0:T(8,128)}, f32[256,128]{1,0:T(8,128)S(1)}, u32[]{:S(2)}, u32[]{:S(2)}) collective-permute-start(f32[256,128]{1,0:T(8,128)} %get-tuple-element.33), channel_id=1, source_target_pairs={{0,4},{1,5},{2,6},{3,7},{4,0},{5,1},{6,2},{7,3},{8,12},{9,13},{10,... | collective-permute-start | bytes 393224 | tf_op jit(solution)/shard_map/ppermute | solution.py:41
  9.8 2.6 %collective-permute-start.6 = (f32[256,128]{1,0:T(8,128)}, f32[256,128]{1,0:T(8,128)S(1)}, u32[]{:S(2)}, u32[]{:S(2)}) collective-permute-start(f32[256,128]{1,0:T(8,128)} %get-tuple-element.34), channel_id=1, source_target_pairs={{0,2},{1,3},{2,4},{3,5},{4,6},{5,7},{6,0},{7,1},{8,10},{9,11},{10,... | collective-permute-start | bytes 393224 | tf_op jit(solution)/shard_map/ppermute | solution.py:41
  12.4 2.5 %collective-permute-done.1.refs_0_ = f32[520,128]{1,0:T(8,128)S(1)} collective-permute-done((f32[520,128]{1,0:T(8,128)S(1)}, f32[520,128]{1,0:T(8,128)S(1)}, u32[]{:S(2)}, u32[]{:S(2)}) %collective-permute-start.1) | collective-permute-done | bytes 266272 | tf_op jit(solution)/shard_map/ppermute | solution.py:41
  14.9 2.2 %collective-permute-start.7 = (f32[256,128]{1,0:T(8,128)S(1)}, f32[256,128]{1,0:T(8,128)S(1)}, u32[]{:S(2)}, u32[]{:S(2)}) collective-permute-start(f32[256,128]{1,0:T(8,128)S(1)} %get-tuple-element.35), channel_id=1, source_target_pairs={{0,6},{1,7},{2,0},{3,1},{4,2},{5,3},{6,4},{7,5},{8,14},{9,15},{10,... | collective-permute-start | bytes 393224 | tf_op jit(solution)/shard_map/ppermute | solution.py:41
  17.1 3.6 %collective-permute-done.2.refs_1_ = f32[520,128]{1,0:T(8,128)S(1)} collective-permute-done((f32[520,128]{1,0:T(8,128)S(1)}, f32[520,128]{1,0:T(8,128)S(1)}, u32[]{:S(2)}, u32[]{:S(2)}) %collective-permute-start.2) | collective-permute-done | bytes 266272 | tf_op jit(solution)/shard_map/ppermute | solution.py:41
  20.7 0.0 collective-permute-start
  20.7 0.0 collective-permute-done.3.refs_2_
  20.7 0.1 pad_maximum_fusion
  20.8 0.6 collective-permute-start.4
  21.3 0.0 copy-done.2
  21.4 0.2 shard_map.47
  21.6 0.8 %collective-permute-done.own_other = f32[776,128]{1,0:T(8,128)S(1)} collective-permute-done((f32[776,128]{1,0:T(8,128)S(1)}, f32[776,128]{1,0:T(8,128)S(1)}, u32[]{:S(2)}, u32[]{:S(2)}) %collective-permute-start) | collective-permute-done | bytes 397344 | tf_op jit(solution)/shard_map/ppermute | solution.py:41
  22.4 1.1 %collective-permute-done.4.refs_3_ = f32[1560,128]{1,0:T(8,128)S(1)} collective-permute-done((f32[1560,128]{1,0:T(8,128)S(1)}, f32[1560,128]{1,0:T(8,128)S(1)}, u32[]{:S(2)}, u32[]{:S(2)}) %collective-permute-start.4) | collective-permute-done | bytes 798752 | tf_op jit(solution)/shard_map/ppermute | solution.py:41
  23.6 0.1 reshape.23.info_ref
  23.7 4.2 %shard_map.48 = (bf16[1024,1024]{1,0:T(8,128)(2,1)S(1)}, bf16[1024,1024]{1,0:T(8,128)(2,1)S(1)}) custom-call(s32[16,3]{1,0:T(8,128)S(1)} %reshape.23.info_ref, bf16[1024,128]{1,0:T(8,128)(2,1)S(1)} %get-tuple-element.30.high_t, bf16[1024,128]{1,0:T(8,128)(2,1)S(1)} %get-tuple-element.31.low_t, f32[776,128]{1,0:T(8,128)S(1)} %get-tuple-element.26.own, ...), custom_call_target="tpu_custom_call" | custom-call | tf_op jit(solution)/shard_map/pallas_call | solution.py:220
  27.8 0.0 collective-permute-done.5.refs_0_
  27.9 0.0 collective-permute-done.6.refs_1_
  27.9 0.0 collective-permute-done.7.refs_2_
  27.9 0.2 collective-permute-start.8
  28.1 1.6 %collective-permute-done.8.refs_3_ = f32[768,128]{1,0:T(8,128)S(1)} collective-permute-done((f32[768,128]{1,0:T(8,128)S(1)}, f32[768,128]{1,0:T(8,128)S(1)}, u32[]{:S(2)}, u32[]{:S(2)}) %collective-permute-start.8) | collective-permute-done | bytes 393248 | tf_op jit(solution)/shard_map/ppermute | solution.py:41
  29.7 2.1 %shard_map.49 = (bf16[1024,512]{1,0:T(8,128)(2,1)S(1)}, bf16[1024,512]{1,0:T(8,128)(2,1)S(1)}) custom-call(s32[16,3]{1,0:T(8,128)S(1)} %reshape.23.info_ref, bf16[1024,128]{1,0:T(8,128)(2,1)S(1)} %get-tuple-element.30.high_t, bf16[1024,128]{1,0:T(8,128)(2,1)S(1)} %get-tuple-element.31.low_t, f32[776,128]{1,0:T(8,128)S(1)} %get-tuple-element.26.own, ...), custom_call_target="tpu_custom_call" | custom-call | tf_op jit(solution)/shard_map/pallas_call | solution.py:220
  31.9 2.9 %shard_map.51 = (f32[1032,128]{1,0:T(8,128)S(1)}, f32[1032,128]{1,0:T(8,128)S(1)}) custom-call(bf16[1024,1024]{1,0:T(8,128)(2,1)S(1)} %get-tuple-element.36.refs_0_, bf16[1024,1024]{1,0:T(8,128)(2,1)S(1)} %get-tuple-element.37.refs_1_, bf16[1024,512]{1,0:T(8,128)(2,1)S(1)} %get-tuple-element.41.refs_2_, bf16[1024,512]{1,0:T(8,128)(2,1)S(1)} %get-tuple-element.42.refs_3_), custom_call_target="tpu_custom_call" | custom-call | flops 2415919104 | tf_op jit(solution)/shard_map/pallas_call | solution.py:238
  34.7 1.9 %collective-permute-start.9 = (f32[1032,128]{1,0:T(8,128)S(1)}, f32[1032,128]{1,0:T(8,128)S(1)}, u32[]{:S(2)}, u32[]{:S(2)}) collective-permute-start(f32[1032,128]{1,0:T(8,128)S(1)} %get-tuple-element.44), channel_id=1, source_target_pairs={{0,4},{1,129},{2,6},{3,131},{4,0},{5,133},{6,2},{7,135},{8,12},{9,... | collective-permute-start | bytes 1585160 | tf_op jit(solution)/shard_map/ppermute | solution.py:41
  36.7 0.9 %collective-permute-start.10 = (f32[1032,128]{1,0:T(8,128)S(1)}, f32[1032,128]{1,0:T(8,128)S(1)}, u32[]{:S(2)}, u32[]{:S(2)}) collective-permute-start(f32[1032,128]{1,0:T(8,128)S(1)} %get-tuple-element.45), channel_id=1, source_target_pairs={{0,2},{1,65},{2,4},{3,67},{4,6},{5,69},{6,0},{7,71},{8,10},{9,73},... | collective-permute-start | bytes 1585160 | tf_op jit(solution)/shard_map/ppermute | solution.py:41
  37.6 2.7 %shard_map.50 = (f32[1024,128]{1,0:T(8,128)S(1)}, f32[1024,128]{1,0:T(8,128)S(1)}) custom-call(bf16[1024,1024]{1,0:T(8,128)(2,1)S(1)} %get-tuple-element.36.refs_0_, bf16[1024,1024]{1,0:T(8,128)(2,1)S(1)} %get-tuple-element.37.refs_1_, bf16[1024,512]{1,0:T(8,128)(2,1)S(1)} %get-tuple-element.41.refs_2_, bf16[1024,512]{1,0:T(8,128)(2,1)S(1)} %get-tuple-element.42.refs_3_), custom_call_target="tpu_custom_call" | custom-call | flops 2415919104 | tf_op jit(solution)/shard_map/pallas_call | solution.py:238
  40.2 1.7 %collective-permute-start.11 = (f32[1024,128]{1,0:T(8,128)S(1)}, f32[1024,128]{1,0:T(8,128)S(1)}, u32[]{:S(2)}, u32[]{:S(2)}) collective-permute-start(f32[1024,128]{1,0:T(8,128)S(1)} %get-tuple-element.46), channel_id=1, source_target_pairs={{0,6},{1,193},{2,0},{3,195},{4,2},{5,197},{6,4},{7,199},{8,14},{9,... | collective-permute-start | bytes 1572872 | tf_op jit(solution)/shard_map/ppermute | solution.py:41
  41.9 9.3 %collective-permute-done.11 = f32[1024,128]{1,0:T(8,128)S(1)} collective-permute-done((f32[1024,128]{1,0:T(8,128)S(1)}, f32[1024,128]{1,0:T(8,128)S(1)}, u32[]{:S(2)}, u32[]{:S(2)}) %collective-permute-start.11) | collective-permute-done | bytes 524320 | tf_op jit(solution)/shard_map/ppermute | solution.py:41
  51.2 0.0 collective-permute-done.9
  51.2 0.9 %collective-permute-done.10 = f32[1032,128]{1,0:T(8,128)S(1)} collective-permute-done((f32[1032,128]{1,0:T(8,128)S(1)}, f32[1032,128]{1,0:T(8,128)S(1)}, u32[]{:S(2)}, u32[]{:S(2)}) %collective-permute-start.10) | collective-permute-done | bytes 528416 | tf_op jit(solution)/shard_map/ppermute | solution.py:41
  52.1 0.2 fusion
  52.3 2.4 %collective-permute-start.12 = (f32[256,128]{1,0:T(8,128)S(1)}, f32[256,128]{1,0:T(8,128)S(1)}, u32[]{:S(2)}, u32[]{:S(2)}) collective-permute-start(f32[256,128]{1,0:T(8,128)S(1)} %get-tuple-element.50), channel_id=1, source_target_pairs={{0,128},{1,5},{2,130},{3,7},{4,132},{5,1},{6,134},{7,3},{8,136},{9... | collective-permute-start | bytes 393224 | tf_op jit(solution)/shard_map/ppermute | solution.py:41
  54.7 1.1 %collective-permute-start.14 = (f32[256,128]{1,0:T(8,128)S(1)}, f32[256,128]{1,0:T(8,128)S(1)}, u32[]{:S(2)}, u32[]{:S(2)}) collective-permute-start(f32[256,128]{1,0:T(8,128)S(1)} %get-tuple-element.51), channel_id=1, source_target_pairs={{0,192},{1,7},{2,194},{3,1},{4,196},{5,3},{6,198},{7,5},{8,200},{9... | collective-permute-start | bytes 393224 | tf_op jit(solution)/shard_map/ppermute | solution.py:41
  55.8 0.9 %collective-permute-start.13 = (f32[256,128]{1,0:T(8,128)S(1)}, f32[256,128]{1,0:T(8,128)S(1)}, u32[]{:S(2)}, u32[]{:S(2)}) collective-permute-start(f32[256,128]{1,0:T(8,128)S(1)} %get-tuple-element.52), channel_id=1, source_target_pairs={{0,64},{1,3},{2,66},{3,5},{4,68},{5,7},{6,70},{7,1},{8,72},{9,11},... | collective-permute-start | bytes 393224 | tf_op jit(solution)/shard_map/ppermute | solution.py:41
  56.7 2.2 %collective-permute-done.12 = f32[256,128]{1,0:T(8,128)S(1)} collective-permute-done((f32[256,128]{1,0:T(8,128)S(1)}, f32[256,128]{1,0:T(8,128)S(1)}, u32[]{:S(2)}, u32[]{:S(2)}) %collective-permute-start.12) | collective-permute-done | bytes 131104 | tf_op jit(solution)/shard_map/ppermute | solution.py:41
  58.9 0.8 collective-permute-done.14
  59.6 2.3 %collective-permute-done.13 = f32[256,128]{1,0:T(8,128)S(1)} collective-permute-done((f32[256,128]{1,0:T(8,128)S(1)}, f32[256,128]{1,0:T(8,128)S(1)}, u32[]{:S(2)}, u32[]{:S(2)}) %collective-permute-start.13) | collective-permute-done | bytes 131104 | tf_op jit(solution)/shard_map/ppermute | solution.py:41
  62.0 17.3 %all_to_all.5 = f32[8,32,128]{2,1,0:T(8,128)S(1)} all-to-all(f32[8,32,128]{2,1,0:T(8,128)S(1)} %bitcast.7), channel_id=1, replica_groups={{0,8,16,24,32,40,48,56},{64,72,80,88,96,104,112,120},{128,136,144,152,1..., dimensions={0} | all-to-all | bytes 262144 | tf_op jit(solution)/shard_map/all_to_all | solution.py:253
  79.4 0.6 reduce_sum.9
  (11 shorter events, 0.1 us)
Async XLA Ops:
  0.7 1.4 %copy-start = (f32[48,2,4096]{2,1,0:T(2,128)S(1)}, f32[48,2,4096]{2,1,0:T(2,128)}, u32[]{:S(2)}) copy-start(f32[48,2,4096]{2,1,0:T(2,128)} %param.4) | copy-start | bytes 4718596
  2.1 0.7 copy-start.1
  2.7 18.6 %copy-start.2 = (f32[128,1024]{1,0:T(8,128)S(1)}, f32[128,1024]{1,0:T(8,128)}, u32[]{:S(2)}) copy-start(f32[128,1024]{1,0:T(8,128)} %orbitals_ref.1) | copy-start | bytes 1572868
  4.1 10.8 %collective-permute-start.1 = (f32[520,128]{1,0:T(8,128)S(1)}, f32[520,128]{1,0:T(8,128)S(1)}, u32[]{:S(2)}, u32[]{:S(2)}) collective-permute-start(f32[520,128]{1,0:T(8,128)S(1)} %get-tuple-element.27), channel_id=1, source_target_pairs={{0,4},{1,5},{2,6},{3,7},{4,0},{5,1},{6,2},{7,3},{8,12},{9,13},{10,... | collective-permute-start | bytes 798728 | tf_op jit(solution)/shard_map/ppermute | solution.py:41
  6.4 14.3 %collective-permute-start.2 = (f32[520,128]{1,0:T(8,128)S(1)}, f32[520,128]{1,0:T(8,128)S(1)}, u32[]{:S(2)}, u32[]{:S(2)}) collective-permute-start(f32[520,128]{1,0:T(8,128)S(1)} %get-tuple-element.28), channel_id=1, source_target_pairs={{0,2},{1,3},{2,4},{3,5},{4,6},{5,7},{6,0},{7,1},{8,10},{9,11},{10,... | collective-permute-start | bytes 798728 | tf_op jit(solution)/shard_map/ppermute | solution.py:41
  7.7 13.0 %collective-permute-start.3 = (f32[520,128]{1,0:T(8,128)S(1)}, f32[520,128]{1,0:T(8,128)S(1)}, u32[]{:S(2)}, u32[]{:S(2)}) collective-permute-start(f32[520,128]{1,0:T(8,128)S(1)} %get-tuple-element.29), channel_id=1, source_target_pairs={{0,6},{1,7},{2,0},{3,1},{4,2},{5,3},{6,4},{7,5},{8,14},{9,15},{10,... | collective-permute-start | bytes 798728 | tf_op jit(solution)/shard_map/ppermute | solution.py:41
  8.4 19.4 %collective-permute-start.5 = (f32[256,128]{1,0:T(8,128)}, f32[256,128]{1,0:T(8,128)S(1)}, u32[]{:S(2)}, u32[]{:S(2)}) collective-permute-start(f32[256,128]{1,0:T(8,128)} %get-tuple-element.33), channel_id=1, source_target_pairs={{0,4},{1,5},{2,6},{3,7},{4,0},{5,1},{6,2},{7,3},{8,12},{9,13},{10,... | collective-permute-start | bytes 393224 | tf_op jit(solution)/shard_map/ppermute | solution.py:41
  9.8 18.1 %collective-permute-start.6 = (f32[256,128]{1,0:T(8,128)}, f32[256,128]{1,0:T(8,128)S(1)}, u32[]{:S(2)}, u32[]{:S(2)}) collective-permute-start(f32[256,128]{1,0:T(8,128)} %get-tuple-element.34), channel_id=1, source_target_pairs={{0,2},{1,3},{2,4},{3,5},{4,6},{5,7},{6,0},{7,1},{8,10},{9,11},{10,... | collective-permute-start | bytes 393224 | tf_op jit(solution)/shard_map/ppermute | solution.py:41
  14.9 13.0 %collective-permute-start.7 = (f32[256,128]{1,0:T(8,128)S(1)}, f32[256,128]{1,0:T(8,128)S(1)}, u32[]{:S(2)}, u32[]{:S(2)}) collective-permute-start(f32[256,128]{1,0:T(8,128)S(1)} %get-tuple-element.35), channel_id=1, source_target_pairs={{0,6},{1,7},{2,0},{3,1},{4,2},{5,3},{6,4},{7,5},{8,14},{9,15},{10,... | collective-permute-start | bytes 393224 | tf_op jit(solution)/shard_map/ppermute | solution.py:41
  20.7 1.7 %collective-permute-start = (f32[776,128]{1,0:T(8,128)S(1)}, f32[776,128]{1,0:T(8,128)S(1)}, u32[]{:S(2)}, u32[]{:S(2)}) collective-permute-start(f32[776,128]{1,0:T(8,128)S(1)} %get-tuple-element.26.own), channel_id=1, source_target_pairs={{0,1},{1,0},{2,3},{3,2},{4,5},{5,4},{6,7},{7,6},{8,9},{9,8},{10,11... | collective-permute-start | bytes 1191944 | tf_op jit(solution)/shard_map/ppermute | solution.py:41
  20.8 2.8 %collective-permute-start.4 = (f32[1560,128]{1,0:T(8,128)S(1)}, f32[1560,128]{1,0:T(8,128)S(1)}, u32[]{:S(2)}, u32[]{:S(2)}) collective-permute-start(f32[1560,128]{1,0:T(8,128)S(1)} %pad_maximum_fusion), channel_id=1, source_target_pairs={{0,1},{1,0},{2,3},{3,2},{4,5},{5,4},{6,7},{7,6},{8,9},{9,8},{10,11... | collective-permute-start | bytes 2396168 | tf_op jit(solution)/shard_map/ppermute | solution.py:41
  27.9 1.8 %collective-permute-start.8 = (f32[768,128]{1,0:T(8,128)S(1)}, f32[768,128]{1,0:T(8,128)S(1)}, u32[]{:S(2)}, u32[]{:S(2)}) collective-permute-start(f32[768,128]{1,0:T(8,128)S(1)} %pad_maximum_fusion.1), channel_id=1, source_target_pairs={{0,1},{1,0},{2,3},{3,2},{4,5},{5,4},{6,7},{7,6},{8,9},{9,8},{10,11... | collective-permute-start | bytes 1179656 | tf_op jit(solution)/shard_map/ppermute | solution.py:41
  34.7 16.4 %collective-permute-start.9 = (f32[1032,128]{1,0:T(8,128)S(1)}, f32[1032,128]{1,0:T(8,128)S(1)}, u32[]{:S(2)}, u32[]{:S(2)}) collective-permute-start(f32[1032,128]{1,0:T(8,128)S(1)} %get-tuple-element.44), channel_id=1, source_target_pairs={{0,4},{1,129},{2,6},{3,131},{4,0},{5,133},{6,2},{7,135},{8,12},{9,... | collective-permute-start | bytes 1585160 | tf_op jit(solution)/shard_map/ppermute | solution.py:41
  36.7 15.4 %collective-permute-start.10 = (f32[1032,128]{1,0:T(8,128)S(1)}, f32[1032,128]{1,0:T(8,128)S(1)}, u32[]{:S(2)}, u32[]{:S(2)}) collective-permute-start(f32[1032,128]{1,0:T(8,128)S(1)} %get-tuple-element.45), channel_id=1, source_target_pairs={{0,2},{1,65},{2,4},{3,67},{4,6},{5,69},{6,0},{7,71},{8,10},{9,73},... | collective-permute-start | bytes 1585160 | tf_op jit(solution)/shard_map/ppermute | solution.py:41
  40.2 10.9 %collective-permute-start.11 = (f32[1024,128]{1,0:T(8,128)S(1)}, f32[1024,128]{1,0:T(8,128)S(1)}, u32[]{:S(2)}, u32[]{:S(2)}) collective-permute-start(f32[1024,128]{1,0:T(8,128)S(1)} %get-tuple-element.46), channel_id=1, source_target_pairs={{0,6},{1,193},{2,0},{3,195},{4,2},{5,197},{6,4},{7,199},{8,14},{9,... | collective-permute-start | bytes 1572872 | tf_op jit(solution)/shard_map/ppermute | solution.py:41
  52.3 6.6 %collective-permute-start.12 = (f32[256,128]{1,0:T(8,128)S(1)}, f32[256,128]{1,0:T(8,128)S(1)}, u32[]{:S(2)}, u32[]{:S(2)}) collective-permute-start(f32[256,128]{1,0:T(8,128)S(1)} %get-tuple-element.50), channel_id=1, source_target_pairs={{0,128},{1,5},{2,130},{3,7},{4,132},{5,1},{6,134},{7,3},{8,136},{9... | collective-permute-start | bytes 393224 | tf_op jit(solution)/shard_map/ppermute | solution.py:41
  54.7 5.0 %collective-permute-start.14 = (f32[256,128]{1,0:T(8,128)S(1)}, f32[256,128]{1,0:T(8,128)S(1)}, u32[]{:S(2)}, u32[]{:S(2)}) collective-permute-start(f32[256,128]{1,0:T(8,128)S(1)} %get-tuple-element.51), channel_id=1, source_target_pairs={{0,192},{1,7},{2,194},{3,1},{4,196},{5,3},{6,198},{7,5},{8,200},{9... | collective-permute-start | bytes 393224 | tf_op jit(solution)/shard_map/ppermute | solution.py:41
  55.8 6.2 %collective-permute-start.13 = (f32[256,128]{1,0:T(8,128)S(1)}, f32[256,128]{1,0:T(8,128)S(1)}, u32[]{:S(2)}, u32[]{:S(2)}) collective-permute-start(f32[256,128]{1,0:T(8,128)S(1)} %get-tuple-element.52), channel_id=1, source_target_pairs={{0,64},{1,3},{2,66},{3,5},{4,68},{5,7},{6,70},{7,1},{8,72},{9,11},... | collective-permute-start | bytes 393224 | tf_op jit(solution)/shard_map/ppermute | solution.py:41

commit v3 on v2

--- a/solution.py
+++ b/solution.py
@@ -14,7 +14,7 @@
 AUX_DEV = 48
 NX, NZ, NY, NC = 4, 8, 4, 2
 CHIP_AUX = AUX_DEV // NY
-CHUNKS = (8, 4)
+CHUNKS = (6, 6)
 STEPS = (2, 1, 3)
 ROWS = BLK // 2
 HEAD = 8
@@ -65,9 +65,11 @@
     lane = lax.broadcasted_iota(jnp.int32, (HEAD, 128), 1)
     head = jnp.zeros((HEAD, 128), F32)
     for slot in range(2):
-        live = (occ * 2 + slot < count_ref[0]).astype(jnp.int32)
-        for j, number in enumerate((pairs_ref[0, slot, 0], pairs_ref[0, slot, 1], live)):
-            head = jnp.where(lane == 3 * slot + j, number.astype(F32), head)
+        live = (occ * 2 + slot < count_ref[0]).astype(jnp.int32).astype(F32)
+        head = jnp.where(lane == 3 * slot + 2, live, head)
+        for j in range(2):
+            number = pairs_ref[0, slot : slot + 1, j : j + 1].astype(F32)
+            head = jnp.where(lane == 3 * slot + j, jnp.broadcast_to(number, head.shape), head)
 
     def fill(out, step, start, count, headed):
         chip = lax.rem(occ // NC + step, NY)
@@ -101,22 +103,26 @@
 
 
 def half_kernel(chunk, info_ref, high_t, low_t, own, own_other, *refs):
-    got, (got_other, high_ref, low_ref, half, parts) = refs[:3], refs[3:]
+    got, refs = refs[:3], refs[3:]
+    got_other, (high_ref, low_ref, half, parts) = refs[:-4], refs[-4:]
     count, head = CHUNKS[chunk], HEAD if chunk == 0 else 0
     sources = [(ref, CHIP_AUX * ROWS, chunk * CHUNKS[0] * ROWS) for ref in (own, own_other)]
     sources += [(ref, count * ROWS, 0) for ref in got]
-    sources += [(got_other, count * ROWS, j * (2 * count * ROWS + head)) for j in range(3)]
+    if chunk == 0:
+        sources += [(got_other[0], count * ROWS, j * (2 * count * ROWS + head)) for j in range(3)]
+    else:
+        sources += [(ref, count * ROWS, 0) for ref in got_other]
     half[...] = jnp.zeros_like(half)
     for source, (ref, stride, start) in enumerate(sources):
         for slot in range(2):
             index = source * 2 + slot
             high, low = split(ref[pl.ds(start + slot * stride, count * ROWS), :])
-            weights = picked(high_t, info_ref, index)
+            weights, rest = (picked(ref, info_ref, index) for ref in (high_t, low_t))
             parts[index] = jnp.dot(
-                jnp.concatenate([high, low], axis=1),
-                jnp.concatenate([weights, weights], axis=0),
+                jnp.concatenate([high, low, high], axis=1),
+                jnp.concatenate([weights, weights, rest], axis=0),
                 preferred_element_type=F32,
-            ) + jnp.dot(high, picked(low_t, info_ref, index), preferred_element_type=F32)
+            )
     for index in range(16):
         row = pl.multiple_of(info_ref[index, 0] * BLK, BLK)
         for q in range(count):
@@ -131,8 +137,8 @@
         low_ref[:, q * 128 : (q + 1) * 128] = low
 
 
-def exchange_kernel(steps, *refs):
-    halves, outs = refs[:4], refs[4:]
+def exchange_kernel(steps, parts, *refs):
+    halves, before, outs = refs[: 2 * parts], refs[2 * parts : -2], refs[-2:]
     aux, occ = lax.axis_index("aux"), lax.axis_index("occ")
     x, y, core = aux // NZ, occ // NC, lax.rem(occ, NC)
 
@@ -144,28 +150,31 @@
         return ref[pl.ds(pl.multiple_of(start, 128), 128), :]
 
     def product(row_steps, column_steps):
-        value = None
-        for part in range(2):
-            high_ref, low_ref = halves[2 * part], halves[2 * part + 1]
-            high, low = (
-                jnp.concatenate([rows(ref, i) for i in row_steps], axis=0)
-                for ref in (high_ref, low_ref)
-            )
-            col_high, col_low = (
-                jnp.concatenate([columns(ref, j) for j in column_steps], axis=0)
-                for ref in (high_ref, low_ref)
-            )
-            for left, right in ((high, col_high), (high, col_low), (low, col_high)):
-                term = lax.dot_general(left, right, NT, preferred_element_type=F32)
-                value = term if value is None else value + term
-        return value
+        high, low = (
+            [jnp.concatenate([rows(ref, i) for i in row_steps], axis=0) for ref in halves[n::2]]
+            for n in range(2)
+        )
+        col_high, col_low = (
+            [jnp.concatenate([columns(ref, j) for j in column_steps], axis=0) for ref in halves[n::2]]
+            for n in range(2)
+        )
+        return lax.dot_general(
+            jnp.concatenate([*high, *high, *low], axis=1),
+            jnp.concatenate([*col_high, *col_low, *col_high], axis=1),
+            NT,
+            preferred_element_type=F32,
+        )
+
+    def put(a, b, tile):
+        spot = slice(b * 256, b * 256 + 256)
+        outs[a][spot] = before[a][spot] + tile if before else tile
 
     @pl.when(core == 0)
     def _():
         value = product(range(NX), steps)
         for a in range(2):
             for b in range(4):
-                outs[a][b * 256 : (b + 1) * 256] = value[b * 256 : (b + 1) * 256, a * 128 : (a + 1) * 128]
+                put(a, b, value[b * 256 : (b + 1) * 256, a * 128 : (a + 1) * 128])
 
     @pl.when(core == 1)
     def _():
@@ -173,9 +182,12 @@
             value = product(steps, (2 * pair, 2 * pair + 1))
             for a in range(2):
                 for b in range(2):
-                    outs[a][(2 * pair + b) * 256 : (2 * pair + b + 1) * 256] = value[
-                        a * 256 : (a + 1) * 256, b * 128 : (b + 1) * 128
-                    ]
+                    put(
+                        a,
+                        2 * pair + b,
+                        value[a * 256 : (a + 1) * 256, b * 128 : (b + 1) * 128],
+                    )
+
     for out in outs:
         if out.shape[0] > 1024:
             out[1024:] = jnp.zeros((out.shape[0] - 1024, 128), F32)
@@ -192,7 +204,7 @@
         [shape((2 * CHIP_AUX * ROWS + HEAD, 128), F32)]
         + [shape((2 * first * ROWS + HEAD, 128), F32)] * 3
         + [shape((2 * second * ROWS, 128), F32)] * 3,
-        [SMEM, SMEM, VMEM],
+        [VMEM, SMEM, VMEM],
     )(pair_list, pair_count, tiles)
     high_t, low_t = call(orbitals_kernel, [shape((NBF, NOCC), BF16)] * 2, [VMEM], flops=ORDER)(orbitals)
 
@@ -220,13 +232,24 @@
         return call(
             functools.partial(half_kernel, chunk),
             [shape((NBF, count * NOCC), BF16)] * 2,
-            [SMEM] + [VMEM] * 8,
+            [SMEM] + [VMEM] * (4 + len(parts)),
             [pltpu.VMEM((count, NBF, NOCC), F32), pltpu.VMEM((16, count * ROWS, 256), F32)],
         )(pairs, high_t, low_t, own, own_other, *parts)
 
+    def partial(steps, halves, before=()):
+        return call(
+            functools.partial(exchange_kernel, steps, len(halves) // 2),
+            [shape((4 * 256 + (0 if 0 in steps else PAD), 128), F32)] * 2,
+            [VMEM] * (len(halves) + len(before)),
+            flops=2 * 3 * 256 * 1024 * CHIP_AUX * NOCC,
+        )(*halves, *before)
+
     halves = list(half(0, *got, got_other))
     halves[0], *later = lax.optimization_barrier((halves[0], *later))
-    halves += half(1, *later, over_core(jnp.concatenate(later)))
+    before = partial((1, 3), halves)
+    last = half(1, *later, *(over_core(part) for part in later))
+    one, three = partial((1, 3), last, before)
+    two, summed = partial((2, 0), [*halves, *last])
 
     def along(k, swapped):
         def where(x, z, y, c):
@@ -234,17 +257,7 @@
 
         return where
 
-    def partial(steps):
-        return call(
-            functools.partial(exchange_kernel, steps),
-            [shape((4 * 256 + (0 if 0 in steps else PAD), 128), F32)] * 2,
-            [VMEM] * 4,
-            flops=2 * 3 * 256 * 1024 * CHIP_AUX * NOCC,
-        )(*halves)
-
-    two, one = partial((2, 1))
-    three, summed = partial((3, 0))
-    for part, k in ((two, 2), (one, 1), (three, 3)):
+    for part, k in ((one, 1), (three, 3), (two, 2)):
         summed += send(part, along(k, False))[:1024]
     summed = summed.reshape(4, 256, 128)
     got = [send(summed[k], along(k, True)) for k in STEPS]

time: 80.2 us -> 78.2 us (0.975)
  waiting for transfers between devices: 25 us -> 22.4 us
  starting transfers between devices: 20.3 us -> 22 us
  Pallas kernels: 13.4 us -> 12.4 us
    ppermute x15 -> x17, waiting for transfers between devices: 25 us -> 22.4 us  [send(): return lax.ppermute(array, ('aux', 'occ'), pairs)]
    ppermute x15 -> x17, starting transfers between devices: 20.3 us -> 22 us  [send(): return lax.ppermute(array, ('aux', 'occ'), pairs)]
    pallas_call x2 -> x3, Pallas kernels: 5.51 us -> 5.68 us  [partial(): call(functools.partial(exchange_kernel, steps, len(halves) // 2), [shape(...]
  transfers between devices with their start and end apart: 15 -> 17, of which waited for: 10 -> 9; matrix products, arithmetic and copies ran while one was open for 0% -> 0% of each run, Pallas kernels for 9% -> 9%
where the time goes in v3:
time: 78.2 us; the launch traced here: 78 us
  waiting for transfers between devices  22.4 us (29%)
  starting transfers between devices  22 us (28%)
  blocking collectives  17.4 us (22%)
  Pallas kernels  12.4 us (16%)
  local copies, waits for them, and re-layouts  2.22 us (3%)
  other arithmetic  0.86 us (1%)
  between operations  0.81 us (1%)
    ppermute x17, waiting for transfers between devices, send(): return lax.ppermute(array, ('aux', 'occ'), pairs)  22.4 us
    ppermute x17, starting transfers between devices, send(): return lax.ppermute(array, ('aux', 'occ'), pairs)  22 us
    all_to_all x1, blocking collectives, per_device(): lax.all_to_all(summed.reshape(NZ, 32, 128), 'aux', 0, 0, axis_index_group...  17.4 us
    pallas_call x2, Pallas kernels, half(): call(functools.partial(half_kernel, chunk), [shape((NBF, count * NOCC), B...  5.69 us
    pallas_call x3, Pallas kernels, partial(): call(functools.partial(exchange_kernel, steps, len(halves) // 2), [shape(...  5.68 us
    unnamed x6, local copies, waits for them, and re-layouts  2.08 us
  transfers between devices with their start and end apart: 17, of which 9 were waited for; matrix products, arithmetic and copies ran while one was open for 0% of the time, Pallas kernels for 9%

profile of v3, /device:TPU:8, one launch (start us, length us, event | category | flops | bytes accessed | tf_op | source)
XLA Modules:
  0.0 78.0 jit_solution(13548326321626576051)
XLA Ops:
  0.7 0.0 copy-start
  0.7 1.4 %copy-done = f32[48,2,4096]{2,1,0:T(2,128)S(1)} copy-done((f32[48,2,4096]{2,1,0:T(2,128)S(1)}, f32[48,2,4096]{2,1,0:T(2,128)}, u32[]{:S(2)}) %copy-start) | copy-done | bytes 1572888
  2.1 0.0 copy-start.1
  2.1 0.7 copy-done.1
  2.7 0.0 copy-start.2
  2.7 0.8 %shard_map.46 = (f32[776,128]{1,0:T(8,128)S(1)}, f32[392,128]{1,0:T(8,128)S(1)}, f32[392,128]{1,0:T(8,128)S(1)}, f32[392,128]{1,0:T(8,128)S(1)}, f32[384,128]{1,...) custom-call(s32[1,2,2]{2,1,0:T(2,128)S(1)} %copy-done.1, s32[1]{0:T(128)S(6)} %copy.5.count_ref, ...), custom_call_target="tpu_custom_call" | custom-call | tf_op jit(solution)/shard_map/pallas_call | solution.py:202
  3.6 2.3 %collective-permute-start.1 = (f32[392,128]{1,0:T(8,128)S(1)}, f32[392,128]{1,0:T(8,128)S(1)}, u32[]{:S(2)}, u32[]{:S(2)}) collective-permute-start(f32[392,128]{1,0:T(8,128)S(1)} %get-tuple-element.29), channel_id=1, source_target_pairs={{0,4},{1,5},{2,6},{3,7},{4,0},{5,1},{6,2},{7,3},{8,12},{9,13},{10,... | collective-permute-start | bytes 602120 | tf_op jit(solution)/shard_map/ppermute | solution.py:41
  5.8 1.4 %collective-permute-start.2 = (f32[392,128]{1,0:T(8,128)S(1)}, f32[392,128]{1,0:T(8,128)S(1)}, u32[]{:S(2)}, u32[]{:S(2)}) collective-permute-start(f32[392,128]{1,0:T(8,128)S(1)} %get-tuple-element.30), channel_id=1, source_target_pairs={{0,2},{1,3},{2,4},{3,5},{4,6},{5,7},{6,0},{7,1},{8,10},{9,11},{10,... | collective-permute-start | bytes 602120 | tf_op jit(solution)/shard_map/ppermute | solution.py:41
  7.2 0.7 collective-permute-start.3
  7.9 1.4 %collective-permute-start.5 = (f32[384,128]{1,0:T(8,128)}, f32[384,128]{1,0:T(8,128)S(1)}, u32[]{:S(2)}, u32[]{:S(2)}) collective-permute-start(f32[384,128]{1,0:T(8,128)} %get-tuple-element.35), channel_id=1, source_target_pairs={{0,4},{1,5},{2,6},{3,7},{4,0},{5,1},{6,2},{7,3},{8,12},{9,13},{10,... | collective-permute-start | bytes 589832 | tf_op jit(solution)/shard_map/ppermute | solution.py:41
  9.3 2.6 %collective-permute-start.6 = (f32[384,128]{1,0:T(8,128)S(1)}, f32[384,128]{1,0:T(8,128)S(1)}, u32[]{:S(2)}, u32[]{:S(2)}) collective-permute-start(f32[384,128]{1,0:T(8,128)S(1)} %get-tuple-element.36), channel_id=1, source_target_pairs={{0,2},{1,3},{2,4},{3,5},{4,6},{5,7},{6,0},{7,1},{8,10},{9,11},{10,... | collective-permute-start | bytes 589832 | tf_op jit(solution)/shard_map/ppermute | solution.py:41
  11.9 1.1 %collective-permute-done.1.refs_0_ = f32[392,128]{1,0:T(8,128)S(1)} collective-permute-done((f32[392,128]{1,0:T(8,128)S(1)}, f32[392,128]{1,0:T(8,128)S(1)}, u32[]{:S(2)}, u32[]{:S(2)}) %collective-permute-start.1) | collective-permute-done | bytes 200736 | tf_op jit(solution)/shard_map/ppermute | solution.py:41
  13.0 2.0 %collective-permute-start.7 = (f32[384,128]{1,0:T(8,128)S(1)}, f32[384,128]{1,0:T(8,128)S(1)}, u32[]{:S(2)}, u32[]{:S(2)}) collective-permute-start(f32[384,128]{1,0:T(8,128)S(1)} %get-tuple-element.37), channel_id=1, source_target_pairs={{0,6},{1,7},{2,0},{3,1},{4,2},{5,3},{6,4},{7,5},{8,14},{9,15},{10,... | collective-permute-start | bytes 589832 | tf_op jit(solution)/shard_map/ppermute | solution.py:41
  15.0 2.4 %collective-permute-done.2.refs_1_ = f32[392,128]{1,0:T(8,128)S(1)} collective-permute-done((f32[392,128]{1,0:T(8,128)S(1)}, f32[392,128]{1,0:T(8,128)S(1)}, u32[]{:S(2)}, u32[]{:S(2)}) %collective-permute-start.2) | collective-permute-done | bytes 200736 | tf_op jit(solution)/shard_map/ppermute | solution.py:41
  17.3 0.0 collective-permute-start
  17.4 0.0 collective-permute-done.3.refs_2_
  17.4 0.6 collective-permute-start.4
  18.0 0.0 copy-done.2
  18.0 0.2 shard_map.47
  18.2 0.8 %collective-permute-done.own_other = f32[776,128]{1,0:T(8,128)S(1)} collective-permute-done((f32[776,128]{1,0:T(8,128)S(1)}, f32[776,128]{1,0:T(8,128)S(1)}, u32[]{:S(2)}, u32[]{:S(2)}) %collective-permute-start) | collective-permute-done | bytes 397344 | tf_op jit(solution)/shard_map/ppermute | solution.py:41
  19.1 0.9 %collective-permute-done.4.refs_3_ = f32[1176,128]{1,0:T(8,128)S(1)} collective-permute-done((f32[1176,128]{1,0:T(8,128)S(1)}, f32[1176,128]{1,0:T(8,128)S(1)}, u32[]{:S(2)}, u32[]{:S(2)}) %collective-permute-start.4) | collective-permute-done | bytes 602144 | tf_op jit(solution)/shard_map/ppermute | solution.py:41
  20.0 0.1 reshape.23.info_ref
  20.0 2.8 %shard_map.48 = (bf16[1024,768]{1,0:T(8,128)(2,1)S(1)}, bf16[1024,768]{1,0:T(8,128)(2,1)S(1)}) custom-call(s32[16,3]{1,0:T(8,128)S(1)} %reshape.23.info_ref, bf16[1024,128]{1,0:T(8,128)(2,1)S(1)} %get-tuple-element.32.high_t, bf16[1024,128]{1,0:T(8,128)(2,1)S(1)} %get-tuple-element.33.low_t, f32[776,128]{1,0:T(8,128)S(1)} %get-tuple-element.28.own, ...), custom_call_target="tpu_custom_call" | custom-call | tf_op jit(solution)/shard_map/pallas_call | solution.py:232
  22.9 0.0 collective-permute-done.5.refs_0_
  22.9 1.8 %collective-permute-done.6.refs_1_ = f32[384,128]{1,0:T(8,128)S(1)} collective-permute-done((f32[384,128]{1,0:T(8,128)S(1)}, f32[384,128]{1,0:T(8,128)S(1)}, u32[]{:S(2)}, u32[]{:S(2)}) %collective-permute-start.6) | collective-permute-done | bytes 196640 | tf_op jit(solution)/shard_map/ppermute | solution.py:41
  24.7 0.0 collective-permute-done.7.refs_2_
  24.7 0.0 collective-permute-start.8
  24.7 0.5 collective-permute-start.9
  25.2 0.0 collective-permute-start.10
  25.2 1.6 %shard_map.51 = (f32[1032,128]{1,0:T(8,128)S(1)}, f32[1032,128]{1,0:T(8,128)S(1)}) custom-call(bf16[1024,768]{1,0:T(8,128)(2,1)S(1)} %get-tuple-element.38.refs_0_, bf16[1024,768]{1,0:T(8,128)(2,1)S(1)} %get-tuple-element.39.refs_1_), custom_call_target="tpu_custom_call" | custom-call | flops 2415919104 | tf_op jit(solution)/shard_map/pallas_call | solution.py:240
  26.8 0.0 collective-permute-done.8.refs_3_
  26.9 0.0 collective-permute-done.9.refs_4_
  26.9 0.0 collective-permute-done.10.refs_5_
  26.9 2.8 %shard_map.49 = (bf16[1024,768]{1,0:T(8,128)(2,1)S(1)}, bf16[1024,768]{1,0:T(8,128)(2,1)S(1)}) custom-call(s32[16,3]{1,0:T(8,128)S(1)} %reshape.23.info_ref, bf16[1024,128]{1,0:T(8,128)(2,1)S(1)} %get-tuple-element.32.high_t, bf16[1024,128]{1,0:T(8,128)(2,1)S(1)} %get-tuple-element.33.low_t, f32[776,128]{1,0:T(8,128)S(1)} %get-tuple-element.28.own, ...), custom_call_target="tpu_custom_call" | custom-call | tf_op jit(solution)/shard_map/pallas_call | solution.py:232
  29.7 1.5 %shard_map.52 = (f32[1032,128]{1,0:T(8,128)S(1)}, f32[1032,128]{1,0:T(8,128)S(1)}) custom-call(bf16[1024,768]{1,0:T(8,128)(2,1)S(1)} %get-tuple-element.43.refs_2_.refs_0_, bf16[1024,768]{1,0:T(8,128)(2,1)S(1)} %get-tuple-element.44.refs_3_.refs_1_, f32[1032,128]{1,0:T(8,128)S(1)} %get-tuple-element.46.refs_2_, f32[1032,128]{1,0:T(8,128)S(1)} %get-tuple-element.47.refs_3_), custom_call_target="tpu_custom_call" | custom-call | flops 2415919104 | tf_op jit(solution)/shard_map/pallas_call | solution.py:240
  31.2 2.2 %collective-permute-start.11 = (f32[1032,128]{1,0:T(8,128)S(1)}, f32[1032,128]{1,0:T(8,128)S(1)}, u32[]{:S(2)}, u32[]{:S(2)}) collective-permute-start(f32[1032,128]{1,0:T(8,128)S(1)} %get-tuple-element.48), channel_id=1, source_target_pairs={{0,2},{1,65},{2,4},{3,67},{4,6},{5,69},{6,0},{7,71},{8,10},{9,73},... | collective-permute-start | bytes 1585160 | tf_op jit(solution)/shard_map/ppermute | solution.py:41
  33.4 0.0 collective-permute-start.12
  33.4 2.6 %shard_map.50 = (f32[1024,128]{1,0:T(8,128)S(1)}, f32[1024,128]{1,0:T(8,128)S(1)}) custom-call(bf16[1024,768]{1,0:T(8,128)(2,1)S(1)} %get-tuple-element.38.refs_0_, bf16[1024,768]{1,0:T(8,128)(2,1)S(1)} %get-tuple-element.39.refs_1_, bf16[1024,768]{1,0:T(8,128)(2,1)S(1)} %get-tuple-element.43.refs_2_.refs_0_, ...), custom_call_target="tpu_custom_call" | custom-call | flops 2415919104 | tf_op jit(solution)/shard_map/pallas_call | solution.py:240
  36.0 3.3 %collective-permute-start.13 = (f32[1024,128]{1,0:T(8,128)S(1)}, f32[1024,128]{1,0:T(8,128)S(1)}, u32[]{:S(2)}, u32[]{:S(2)}) collective-permute-start(f32[1024,128]{1,0:T(8,128)S(1)} %get-tuple-element.50), channel_id=1, source_target_pairs={{0,4},{1,129},{2,6},{3,131},{4,0},{5,133},{6,2},{7,135},{8,12},{9,... | collective-permute-start | bytes 1572872 | tf_op jit(solution)/shard_map/ppermute | solution.py:41
  39.3 10.1 %collective-permute-done.13 = f32[1024,128]{1,0:T(8,128)S(1)} collective-permute-done((f32[1024,128]{1,0:T(8,128)S(1)}, f32[1024,128]{1,0:T(8,128)S(1)}, u32[]{:S(2)}, u32[]{:S(2)}) %collective-permute-start.13) | collective-permute-done | bytes 524320 | tf_op jit(solution)/shard_map/ppermute | solution.py:41
  49.4 0.0 collective-permute-done.11
  49.4 0.0 collective-permute-done.12
  49.4 0.2 fusion
  49.6 3.1 %collective-permute-start.14 = (f32[256,128]{1,0:T(8,128)S(1)}, f32[256,128]{1,0:T(8,128)S(1)}, u32[]{:S(2)}, u32[]{:S(2)}) collective-permute-start(f32[256,128]{1,0:T(8,128)S(1)} %get-tuple-element.54), channel_id=1, source_target_pairs={{0,128},{1,5},{2,130},{3,7},{4,132},{5,1},{6,134},{7,3},{8,136},{9... | collective-permute-start | bytes 393224 | tf_op jit(solution)/shard_map/ppermute | solution.py:41
  52.7 1.1 %collective-permute-start.16 = (f32[256,128]{1,0:T(8,128)S(1)}, f32[256,128]{1,0:T(8,128)S(1)}, u32[]{:S(2)}, u32[]{:S(2)}) collective-permute-start(f32[256,128]{1,0:T(8,128)S(1)} %get-tuple-element.55), channel_id=1, source_target_pairs={{0,192},{1,7},{2,194},{3,1},{4,196},{5,3},{6,198},{7,5},{8,200},{9... | collective-permute-start | bytes 393224 | tf_op jit(solution)/shard_map/ppermute | solution.py:41
  53.8 0.9 %collective-permute-start.15 = (f32[256,128]{1,0:T(8,128)S(1)}, f32[256,128]{1,0:T(8,128)S(1)}, u32[]{:S(2)}, u32[]{:S(2)}) collective-permute-start(f32[256,128]{1,0:T(8,128)S(1)} %get-tuple-element.56), channel_id=1, source_target_pairs={{0,64},{1,3},{2,66},{3,5},{4,68},{5,7},{6,70},{7,1},{8,72},{9,11},... | collective-permute-start | bytes 393224 | tf_op jit(solution)/shard_map/ppermute | solution.py:41
  54.7 1.4 %collective-permute-done.14 = f32[256,128]{1,0:T(8,128)S(1)} collective-permute-done((f32[256,128]{1,0:T(8,128)S(1)}, f32[256,128]{1,0:T(8,128)S(1)}, u32[]{:S(2)}, u32[]{:S(2)}) %collective-permute-start.14) | collective-permute-done | bytes 131104 | tf_op jit(solution)/shard_map/ppermute | solution.py:41
  56.1 1.5 %collective-permute-done.16 = f32[256,128]{1,0:T(8,128)S(1)} collective-permute-done((f32[256,128]{1,0:T(8,128)S(1)}, f32[256,128]{1,0:T(8,128)S(1)}, u32[]{:S(2)}, u32[]{:S(2)}) %collective-permute-start.16) | collective-permute-done | bytes 131104 | tf_op jit(solution)/shard_map/ppermute | solution.py:41
  57.7 2.3 %collective-permute-done.15 = f32[256,128]{1,0:T(8,128)S(1)} collective-permute-done((f32[256,128]{1,0:T(8,128)S(1)}, f32[256,128]{1,0:T(8,128)S(1)}, u32[]{:S(2)}, u32[]{:S(2)}) %collective-permute-start.15) | collective-permute-done | bytes 131104 | tf_op jit(solution)/shard_map/ppermute | solution.py:41
  60.1 17.4 %all_to_all.5 = f32[8,32,128]{2,1,0:T(8,128)S(1)} all-to-all(f32[8,32,128]{2,1,0:T(8,128)S(1)} %bitcast.7), channel_id=1, replica_groups={{0,8,16,24,32,40,48,56},{64,72,80,88,96,104,112,120},{128,136,144,152,1..., dimensions={0} | all-to-all | bytes 262144 | tf_op jit(solution)/shard_map/all_to_all | solution.py:266
  77.4 0.6 reduce_sum.9
  (11 shorter events, 0.2 us)
Async XLA Ops:
  0.7 1.4 %copy-start = (f32[48,2,4096]{2,1,0:T(2,128)S(1)}, f32[48,2,4096]{2,1,0:T(2,128)}, u32[]{:S(2)}) copy-start(f32[48,2,4096]{2,1,0:T(2,128)} %param.4) | copy-start | bytes 4718596
  2.1 0.7 copy-start.1
  2.7 15.3 %copy-start.2 = (f32[128,1024]{1,0:T(8,128)S(1)}, f32[128,1024]{1,0:T(8,128)}, u32[]{:S(2)}) copy-start(f32[128,1024]{1,0:T(8,128)} %orbitals_ref.1) | copy-start | bytes 1572868
  3.6 9.4 %collective-permute-start.1 = (f32[392,128]{1,0:T(8,128)S(1)}, f32[392,128]{1,0:T(8,128)S(1)}, u32[]{:S(2)}, u32[]{:S(2)}) collective-permute-start(f32[392,128]{1,0:T(8,128)S(1)} %get-tuple-element.29), channel_id=1, source_target_pairs={{0,4},{1,5},{2,6},{3,7},{4,0},{5,1},{6,2},{7,3},{8,12},{9,13},{10,... | collective-permute-start | bytes 602120 | tf_op jit(solution)/shard_map/ppermute | solution.py:41
  5.8 11.5 %collective-permute-start.2 = (f32[392,128]{1,0:T(8,128)S(1)}, f32[392,128]{1,0:T(8,128)S(1)}, u32[]{:S(2)}, u32[]{:S(2)}) collective-permute-start(f32[392,128]{1,0:T(8,128)S(1)} %get-tuple-element.30), channel_id=1, source_target_pairs={{0,2},{1,3},{2,4},{3,5},{4,6},{5,7},{6,0},{7,1},{8,10},{9,11},{10,... | collective-permute-start | bytes 602120 | tf_op jit(solution)/shard_map/ppermute | solution.py:41
  7.2 10.2 %collective-permute-start.3 = (f32[392,128]{1,0:T(8,128)S(1)}, f32[392,128]{1,0:T(8,128)S(1)}, u32[]{:S(2)}, u32[]{:S(2)}) collective-permute-start(f32[392,128]{1,0:T(8,128)S(1)} %get-tuple-element.31), channel_id=1, source_target_pairs={{0,6},{1,7},{2,0},{3,1},{4,2},{5,3},{6,4},{7,5},{8,14},{9,15},{10,... | collective-permute-start | bytes 602120 | tf_op jit(solution)/shard_map/ppermute | solution.py:41
  7.9 15.0 %collective-permute-start.5 = (f32[384,128]{1,0:T(8,128)}, f32[384,128]{1,0:T(8,128)S(1)}, u32[]{:S(2)}, u32[]{:S(2)}) collective-permute-start(f32[384,128]{1,0:T(8,128)} %get-tuple-element.35), channel_id=1, source_target_pairs={{0,4},{1,5},{2,6},{3,7},{4,0},{5,1},{6,2},{7,3},{8,12},{9,13},{10,... | collective-permute-start | bytes 589832 | tf_op jit(solution)/shard_map/ppermute | solution.py:41
  9.3 15.4 %collective-permute-start.6 = (f32[384,128]{1,0:T(8,128)S(1)}, f32[384,128]{1,0:T(8,128)S(1)}, u32[]{:S(2)}, u32[]{:S(2)}) collective-permute-start(f32[384,128]{1,0:T(8,128)S(1)} %get-tuple-element.36), channel_id=1, source_target_pairs={{0,2},{1,3},{2,4},{3,5},{4,6},{5,7},{6,0},{7,1},{8,10},{9,11},{10,... | collective-permute-start | bytes 589832 | tf_op jit(solution)/shard_map/ppermute | solution.py:41
  13.0 11.7 %collective-permute-start.7 = (f32[384,128]{1,0:T(8,128)S(1)}, f32[384,128]{1,0:T(8,128)S(1)}, u32[]{:S(2)}, u32[]{:S(2)}) collective-permute-start(f32[384,128]{1,0:T(8,128)S(1)} %get-tuple-element.37), channel_id=1, source_target_pairs={{0,6},{1,7},{2,0},{3,1},{4,2},{5,3},{6,4},{7,5},{8,14},{9,15},{10,... | collective-permute-start | bytes 589832 | tf_op jit(solution)/shard_map/ppermute | solution.py:41
  17.3 1.7 %collective-permute-start = (f32[776,128]{1,0:T(8,128)S(1)}, f32[776,128]{1,0:T(8,128)S(1)}, u32[]{:S(2)}, u32[]{:S(2)}) collective-permute-start(f32[776,128]{1,0:T(8,128)S(1)} %get-tuple-element.28.own), channel_id=1, source_target_pairs={{0,1},{1,0},{2,3},{3,2},{4,5},{5,4},{6,7},{7,6},{8,9},{9,8},{10,11... | collective-permute-start | bytes 1191944 | tf_op jit(solution)/shard_map/ppermute | solution.py:41
  17.4 2.5 %collective-permute-start.4 = (f32[1176,128]{1,0:T(8,128)S(1)}, f32[1176,128]{1,0:T(8,128)S(1)}, u32[]{:S(2)}, u32[]{:S(2)}) collective-permute-start(f32[1176,128]{1,0:T(8,128)S(1)} %pad_maximum_fusion), channel_id=1, source_target_pairs={{0,1},{1,0},{2,3},{3,2},{4,5},{5,4},{6,7},{7,6},{8,9},{9,8},{10,11... | collective-permute-start | bytes 1806344 | tf_op jit(solution)/shard_map/ppermute | solution.py:41
  24.7 2.1 %collective-permute-start.8 = (f32[384,128]{1,0:T(8,128)S(1)}, f32[384,128]{1,0:T(8,128)S(1)}, u32[]{:S(2)}, u32[]{:S(2)}) collective-permute-start(f32[384,128]{1,0:T(8,128)S(1)} %collective-permute-done.5.refs_0_), channel_id=1, source_target_pairs={{0,1},{1,0},{2,3},{3,2},{4,5},{5,4},{6,7},{7,6},{8,9},{9,8},{10,11... | collective-permute-start | bytes 589832 | tf_op jit(solution)/shard_map/ppermute | solution.py:41
  24.7 2.1 %collective-permute-start.9 = (f32[384,128]{1,0:T(8,128)S(1)}, f32[384,128]{1,0:T(8,128)S(1)}, u32[]{:S(2)}, u32[]{:S(2)}) collective-permute-start(f32[384,128]{1,0:T(8,128)S(1)} %collective-permute-done.6.refs_1_), channel_id=1, source_target_pairs={{0,1},{1,0},{2,3},{3,2},{4,5},{5,4},{6,7},{7,6},{8,9},{9,8},{10,11... | collective-permute-start | bytes 589832 | tf_op jit(solution)/shard_map/ppermute | solution.py:41
  25.2 1.6 %collective-permute-start.10 = (f32[384,128]{1,0:T(8,128)S(1)}, f32[384,128]{1,0:T(8,128)S(1)}, u32[]{:S(2)}, u32[]{:S(2)}) collective-permute-start(f32[384,128]{1,0:T(8,128)S(1)} %collective-permute-done.7.refs_2_), channel_id=1, source_target_pairs={{0,1},{1,0},{2,3},{3,2},{4,5},{5,4},{6,7},{7,6},{8,9},{9,8},{10,11... | collective-permute-start | bytes 589832 | tf_op jit(solution)/shard_map/ppermute | solution.py:41
  31.2 18.2 %collective-permute-start.11 = (f32[1032,128]{1,0:T(8,128)S(1)}, f32[1032,128]{1,0:T(8,128)S(1)}, u32[]{:S(2)}, u32[]{:S(2)}) collective-permute-start(f32[1032,128]{1,0:T(8,128)S(1)} %get-tuple-element.48), channel_id=1, source_target_pairs={{0,2},{1,65},{2,4},{3,67},{4,6},{5,69},{6,0},{7,71},{8,10},{9,73},... | collective-permute-start | bytes 1585160 | tf_op jit(solution)/shard_map/ppermute | solution.py:41
  33.4 16.0 %collective-permute-start.12 = (f32[1032,128]{1,0:T(8,128)S(1)}, f32[1032,128]{1,0:T(8,128)S(1)}, u32[]{:S(2)}, u32[]{:S(2)}) collective-permute-start(f32[1032,128]{1,0:T(8,128)S(1)} %get-tuple-element.49), channel_id=1, source_target_pairs={{0,6},{1,193},{2,0},{3,195},{4,2},{5,197},{6,4},{7,199},{8,14},{9,... | collective-permute-start | bytes 1585160 | tf_op jit(solution)/shard_map/ppermute | solution.py:41
  36.0 13.4 %collective-permute-start.13 = (f32[1024,128]{1,0:T(8,128)S(1)}, f32[1024,128]{1,0:T(8,128)S(1)}, u32[]{:S(2)}, u32[]{:S(2)}) collective-permute-start(f32[1024,128]{1,0:T(8,128)S(1)} %get-tuple-element.50), channel_id=1, source_target_pairs={{0,4},{1,129},{2,6},{3,131},{4,0},{5,133},{6,2},{7,135},{8,12},{9,... | collective-permute-start | bytes 1572872 | tf_op jit(solution)/shard_map/ppermute | solution.py:41
  49.6 6.6 %collective-permute-start.14 = (f32[256,128]{1,0:T(8,128)S(1)}, f32[256,128]{1,0:T(8,128)S(1)}, u32[]{:S(2)}, u32[]{:S(2)}) collective-permute-start(f32[256,128]{1,0:T(8,128)S(1)} %get-tuple-element.54), channel_id=1, source_target_pairs={{0,128},{1,5},{2,130},{3,7},{4,132},{5,1},{6,134},{7,3},{8,136},{9... | collective-permute-start | bytes 393224 | tf_op jit(solution)/shard_map/ppermute | solution.py:41
  52.7 5.0 %collective-permute-start.16 = (f32[256,128]{1,0:T(8,128)S(1)}, f32[256,128]{1,0:T(8,128)S(1)}, u32[]{:S(2)}, u32[]{:S(2)}) collective-permute-start(f32[256,128]{1,0:T(8,128)S(1)} %get-tuple-element.55), channel_id=1, source_target_pairs={{0,192},{1,7},{2,194},{3,1},{4,196},{5,3},{6,198},{7,5},{8,200},{9... | collective-permute-start | bytes 393224 | tf_op jit(solution)/shard_map/ppermute | solution.py:41
  53.8 6.2 %collective-permute-start.15 = (f32[256,128]{1,0:T(8,128)S(1)}, f32[256,128]{1,0:T(8,128)S(1)}, u32[]{:S(2)}, u32[]{:S(2)}) collective-permute-start(f32[256,128]{1,0:T(8,128)S(1)} %get-tuple-element.56), channel_id=1, source_target_pairs={{0,64},{1,3},{2,66},{3,5},{4,68},{5,7},{6,70},{7,1},{8,72},{9,11},... | collective-permute-start | bytes 393224 | tf_op jit(solution)/shard_map/ppermute | solution.py:41

commit v4 on v3

--- a/solution.py
+++ b/solution.py
@@ -20,6 +20,10 @@
 HEAD = 8
 ORDER = 10**11
 PAD = 8
+PLACES = {
+    (2, 1): ((((0, 0), (1, 0)), ((2, 0), (0, 512))), (1024 + PAD, 512 + PAD, 512)),
+    (3, 0): ((((0, 0), (0, 512)), ((1, 0), (1, 512))), (1024, 1024)),
+}
 VMEM = pl.BlockSpec(memory_space=pltpu.VMEM)
 SMEM = pl.BlockSpec(memory_space=pltpu.SMEM)
 F32, BF16 = jnp.float32, jnp.bfloat16
@@ -138,7 +142,9 @@
 
 
 def exchange_kernel(steps, parts, *refs):
-    halves, before, outs = refs[: 2 * parts], refs[2 * parts : -2], refs[-2:]
+    place, sizes = PLACES[steps]
+    count = len(sizes)
+    halves, before, outs = refs[: 2 * parts], refs[2 * parts : -count], refs[-count:]
     aux, occ = lax.axis_index("aux"), lax.axis_index("occ")
     x, y, core = aux // NZ, occ // NC, lax.rem(occ, NC)
 
@@ -166,8 +172,10 @@
         )
 
     def put(a, b, tile):
-        spot = slice(b * 256, b * 256 + 256)
-        outs[a][spot] = before[a][spot] + tile if before else tile
+        which, start = place[a][b // 2]
+        start += b % 2 * 256
+        spot = slice(start, start + 256)
+        outs[which][spot] = before[which][spot] + tile if before else tile
 
     @pl.when(core == 0)
     def _():
@@ -189,8 +197,8 @@
                     )
 
     for out in outs:
-        if out.shape[0] > 1024:
-            out[1024:] = jnp.zeros((out.shape[0] - 1024, 128), F32)
+        if out.shape[0] % 512:
+            out[-PAD:] = jnp.zeros((PAD, 128), F32)
 
 
 def per_device(blocks, pair_list, pair_count, orbitals):
@@ -239,17 +247,17 @@
     def partial(steps, halves, before=()):
         return call(
             functools.partial(exchange_kernel, steps, len(halves) // 2),
-            [shape((4 * 256 + (0 if 0 in steps else PAD), 128), F32)] * 2,
+            [shape((size, 128), F32) for size in PLACES[steps][1]],
             [VMEM] * (len(halves) + len(before)),
             flops=2 * 3 * 256 * 1024 * CHIP_AUX * NOCC,
         )(*halves, *before)
 
     halves = list(half(0, *got, got_other))
     halves[0], *later = lax.optimization_barrier((halves[0], *later))
-    before = partial((1, 3), halves)
+    before = partial((2, 1), halves)
     last = half(1, *later, *(over_core(part) for part in later))
-    one, three = partial((1, 3), last, before)
-    two, summed = partial((2, 0), [*halves, *last])
+    right, left, one_a = partial((2, 1), last, before)
+    three, own_part = partial((3, 0), [*halves, *last])
 
     def along(k, swapped):
         def where(x, z, y, c):
@@ -257,11 +265,15 @@
 
         return where
 
-    for part, k in ((one, 1), (three, 3), (two, 2)):
-        summed += send(part, along(k, False))[:1024]
-    summed = summed.reshape(4, 256, 128)
-    got = [send(summed[k], along(k, True)) for k in STEPS]
-    summed = summed[0] + got[0] + got[1] + got[2]
+    right, left = send(right, along(1, False)), send(left, along(3, False))
+    three = send(jnp.concatenate([three[:512], three[512:] + left[:512]]), along(3, False))
+    one_a = send(one_a + right[:512], along(1, False))
+    three, one_a = lax.optimization_barrier((three, one_a))
+    three += own_part
+    summed = (three[:512] + one_a, three[512:] + right[512:1024])
+    tiles = [tile for part in summed for tile in (part[:256], part[256:])]
+    got = [send(tiles[k], along(k, True)) for k in STEPS]
+    summed = tiles[0] + got[0] + got[1] + got[2]
     groups = [[a * NZ + b for b in range(NZ)] for a in range(NX)]
     parts = lax.all_to_all(
         summed.reshape(NZ, 32, 128), "aux", 0, 0, axis_index_groups=groups, tiled=True

time: 78.2 us -> 83.7 us (1.070)
  the two profiles are of different devices: /device:TPU:8 before, /device:TPU:6 now
where the time goes in v4:
time: 83.7 us; the launch traced here: 83.6 us
  waiting for transfers between devices  25.7 us (31%)
  starting transfers between devices  24.1 us (29%)
  blocking collectives  17.3 us (21%)
  Pallas kernels  12.4 us (15%)
  local copies, waits for them, and re-layouts  2.23 us (3%)
  other arithmetic  0.95 us (1%)
  between operations  0.86 us (1%)
    ppermute x18, waiting for transfers between devices, send(): return lax.ppermute(array, ('aux', 'occ'), pairs)  25.7 us
    ppermute x18, starting transfers between devices, send(): return lax.ppermute(array, ('aux', 'occ'), pairs)  24.1 us
    all_to_all x1, blocking collectives, per_device(): lax.all_to_all(summed.reshape(NZ, 32, 128), 'aux', 0, 0, axis_index_group...  17.3 us
    pallas_call x2, Pallas kernels, half(): call(functools.partial(half_kernel, chunk), [shape((NBF, count * NOCC), B...  5.69 us
    pallas_call x3, Pallas kernels, partial(): call(functools.partial(exchange_kernel, steps, len(halves) // 2), [shape(...  5.68 us
    unnamed x6, local copies, waits for them, and re-layouts  2.08 us
  transfers between devices with their start and end apart: 18, of which 11 were waited for; matrix products, arithmetic and copies ran while one was open for 0% of the time, Pallas kernels for 9%

profile of v4, /device:TPU:6, one launch (start us, length us, event | category | flops | bytes accessed | tf_op | source)
XLA Modules:
  0.0 83.6 jit_solution(11422960477581482708)
XLA Ops:
  0.7 0.0 copy-start
  0.7 1.4 %copy-done = f32[48,2,4096]{2,1,0:T(2,128)S(1)} copy-done((f32[48,2,4096]{2,1,0:T(2,128)S(1)}, f32[48,2,4096]{2,1,0:T(2,128)}, u32[]{:S(2)}) %copy-start) | copy-done | bytes 1572888
  2.1 0.0 copy-start.1
  2.1 0.7 copy-done.1
  2.7 0.0 copy-start.2
  2.7 0.8 shard_map.46
  3.6 3.2 %collective-permute-start.1 = (f32[392,128]{1,0:T(8,128)S(1)}, f32[392,128]{1,0:T(8,128)S(1)}, u32[]{:S(2)}, u32[]{:S(2)}) collective-permute-start(f32[392,128]{1,0:T(8,128)S(1)} %get-tuple-element.33), channel_id=1, source_target_pairs={{0,4},{1,5},{2,6},{3,7},{4,0},{5,1},{6,2},{7,3},{8,12},{9,13},{10,... | collective-permute-start | bytes 602120 | tf_op jit(solution)/shard_map/ppermute | solution.py:45
  6.8 0.7 collective-permute-start.2
  7.4 2.6 %collective-permute-start.3 = (f32[392,128]{1,0:T(8,128)S(1)}, f32[392,128]{1,0:T(8,128)S(1)}, u32[]{:S(2)}, u32[]{:S(2)}) collective-permute-start(f32[392,128]{1,0:T(8,128)S(1)} %get-tuple-element.35), channel_id=1, source_target_pairs={{0,6},{1,7},{2,0},{3,1},{4,2},{5,3},{6,4},{7,5},{8,14},{9,15},{10,... | collective-permute-start | bytes 602120 | tf_op jit(solution)/shard_map/ppermute | solution.py:45
  10.0 0.0 collective-permute-start.5
  10.0 0.9 %collective-permute-start.6 = (f32[384,128]{1,0:T(8,128)S(1)}, f32[384,128]{1,0:T(8,128)S(1)}, u32[]{:S(2)}, u32[]{:S(2)}) collective-permute-start(f32[384,128]{1,0:T(8,128)S(1)} %get-tuple-element.40), channel_id=1, source_target_pairs={{0,2},{1,3},{2,4},{3,5},{4,6},{5,7},{6,0},{7,1},{8,10},{9,11},{10,... | collective-permute-start | bytes 589832 | tf_op jit(solution)/shard_map/ppermute | solution.py:45
  10.8 2.1 %collective-permute-done.1.refs_0_ = f32[392,128]{1,0:T(8,128)S(1)} collective-permute-done((f32[392,128]{1,0:T(8,128)S(1)}, f32[392,128]{1,0:T(8,128)S(1)}, u32[]{:S(2)}, u32[]{:S(2)}) %collective-permute-start.1) | collective-permute-done | bytes 200736 | tf_op jit(solution)/shard_map/ppermute | solution.py:45
  12.9 3.0 %collective-permute-start.7 = (f32[384,128]{1,0:T(8,128)S(1)}, f32[384,128]{1,0:T(8,128)S(1)}, u32[]{:S(2)}, u32[]{:S(2)}) collective-permute-start(f32[384,128]{1,0:T(8,128)S(1)} %get-tuple-element.41), channel_id=1, source_target_pairs={{0,6},{1,7},{2,0},{3,1},{4,2},{5,3},{6,4},{7,5},{8,14},{9,15},{10,... | collective-permute-start | bytes 589832 | tf_op jit(solution)/shard_map/ppermute | solution.py:45
  16.0 4.1 %collective-permute-done.2.refs_1_ = f32[392,128]{1,0:T(8,128)S(1)} collective-permute-done((f32[392,128]{1,0:T(8,128)S(1)}, f32[392,128]{1,0:T(8,128)S(1)}, u32[]{:S(2)}, u32[]{:S(2)}) %collective-permute-start.2) | collective-permute-done | bytes 200736 | tf_op jit(solution)/shard_map/ppermute | solution.py:45
  20.1 0.0 collective-permute-start
  20.1 0.0 collective-permute-done.3.refs_2_
  20.1 0.6 collective-permute-start.4
  20.7 0.0 copy-done.2
  20.7 0.2 shard_map.47
  21.0 0.8 collective-permute-done.own_other
  21.8 0.9 %collective-permute-done.4.refs_3_ = f32[1176,128]{1,0:T(8,128)S(1)} collective-permute-done((f32[1176,128]{1,0:T(8,128)S(1)}, f32[1176,128]{1,0:T(8,128)S(1)}, u32[]{:S(2)}, u32[]{:S(2)}) %collective-permute-start.4) | collective-permute-done | bytes 602144 | tf_op jit(solution)/shard_map/ppermute | solution.py:45
  22.7 0.1 reshape.14.info_ref
  22.8 2.8 %shard_map.48 = (bf16[1024,768]{1,0:T(8,128)(2,1)S(1)}, bf16[1024,768]{1,0:T(8,128)(2,1)S(1)}) custom-call(s32[16,3]{1,0:T(8,128)S(1)} %reshape.14.info_ref, bf16[1024,128]{1,0:T(8,128)(2,1)S(1)} %get-tuple-element.36.high_t, bf16[1024,128]{1,0:T(8,128)(2,1)S(1)} %get-tuple-element.37.low_t, f32[776,128]{1,0:T(8,128)S(1)} %get-tuple-element.32.own, ...), custom_call_target="tpu_custom_call" | custom-call | tf_op jit(solution)/shard_map/pallas_call | solution.py:240
  25.7 0.0 collective-permute-done.5.refs_0_
  25.7 0.0 collective-permute-done.6.refs_1_
  25.7 0.0 collective-permute-done.7.refs_2_
  25.7 0.2 collective-permute-start.8
  25.9 0.4 collective-permute-start.9
  26.3 0.1 collective-permute-start.10
  26.4 1.6 %shard_map.51 = (f32[1032,128]{1,0:T(8,128)S(1)}, f32[520,128]{1,0:T(8,128)S(1)}, f32[512,128]{1,0:T(8,128)S(1)}) custom-call(bf16[1024,768]{1,0:T(8,128)(2,1)S(1)} %get-tuple-element.42.refs_0_, bf16[1024,768]{1,0:T(8,128)(2,1)S(1)} %get-tuple-element.43.refs_1_), custom_call_target="tpu_custom_call" | custom-call | flops 2415919104 | tf_op jit(solution)/shard_map/pallas_call | solution.py:248
  28.0 0.0 collective-permute-done.8.refs_3_
  28.0 0.0 collective-permute-done.9.refs_4_
  28.0 0.0 collective-permute-done.10.refs_5_
  28.1 2.8 %shard_map.49 = (bf16[1024,768]{1,0:T(8,128)(2,1)S(1)}, bf16[1024,768]{1,0:T(8,128)(2,1)S(1)}) custom-call(s32[16,3]{1,0:T(8,128)S(1)} %reshape.14.info_ref, bf16[1024,128]{1,0:T(8,128)(2,1)S(1)} %get-tuple-element.36.high_t, bf16[1024,128]{1,0:T(8,128)(2,1)S(1)} %get-tuple-element.37.low_t, f32[776,128]{1,0:T(8,128)S(1)} %get-tuple-element.32.own, ...), custom_call_target="tpu_custom_call" | custom-call | tf_op jit(solution)/shard_map/pallas_call | solution.py:240
  30.9 1.5 %shard_map.52 = (f32[1032,128]{1,0:T(8,128)S(1)}, f32[520,128]{1,0:T(8,128)S(1)}, f32[512,128]{1,0:T(8,128)S(1)}) custom-call(bf16[1024,768]{1,0:T(8,128)(2,1)S(1)} %get-tuple-element.47.refs_2_.refs_0_, bf16[1024,768]{1,0:T(8,128)(2,1)S(1)} %get-tuple-element.48.refs_3_.refs_1_, f32[1032,128]{1,0:T(8,128)S(1)} %get-tuple-element.50.refs_2_, ...), custom_call_target="tpu_custom_call" | custom-call | flops 2415919104 | tf_op jit(solution)/shard_map/pallas_call | solution.py:248
  32.4 2.9 %collective-permute-start.11 = (f32[520,128]{1,0:T(8,128)S(1)}, f32[520,128]{1,0:T(8,128)S(1)}, u32[]{:S(2)}, u32[]{:S(2)}) collective-permute-start(f32[520,128]{1,0:T(8,128)S(1)} %get-tuple-element.53), channel_id=1, source_target_pairs={{0,6},{1,193},{2,0},{3,195},{4,2},{5,197},{6,4},{7,199},{8,14},{9,... | collective-permute-start | bytes 798728 | tf_op jit(solution)/shard_map/ppermute | solution.py:45
  35.3 0.0 collective-permute-start.13
  35.3 2.6 %shard_map.50 = (f32[1024,128]{1,0:T(8,128)S(1)}, f32[1024,128]{1,0:T(8,128)S(1)}) custom-call(bf16[1024,768]{1,0:T(8,128)(2,1)S(1)} %get-tuple-element.42.refs_0_, bf16[1024,768]{1,0:T(8,128)(2,1)S(1)} %get-tuple-element.43.refs_1_, bf16[1024,768]{1,0:T(8,128)(2,1)S(1)} %get-tuple-element.47.refs_2_.refs_0_, ...), custom_call_target="tpu_custom_call" | custom-call | flops 2415919104 | tf_op jit(solution)/shard_map/pallas_call | solution.py:248
  37.9 1.3 %collective-permute-done.11 = f32[520,128]{1,0:T(8,128)S(1)} collective-permute-done((f32[520,128]{1,0:T(8,128)S(1)}, f32[520,128]{1,0:T(8,128)S(1)}, u32[]{:S(2)}, u32[]{:S(2)}) %collective-permute-start.11) | collective-permute-done | bytes 266272 | tf_op jit(solution)/shard_map/ppermute | solution.py:45
  39.3 3.8 %collective-permute-start.12 = (f32[1024,128]{1,0:T(8,128)S(1)}, f32[1024,128]{1,0:T(8,128)S(1)}, u32[]{:S(2)}, u32[]{:S(2)}) collective-permute-start(f32[1024,128]{1,0:T(8,128)S(1)} %pad_maximum_fusion.1), channel_id=1, source_target_pairs={{0,6},{1,193},{2,0},{3,195},{4,2},{5,197},{6,4},{7,199},{8,14},{9,... | collective-permute-start | bytes 1572872 | tf_op jit(solution)/shard_map/ppermute | solution.py:45
  43.1 2.6 %collective-permute-done.13 = f32[1032,128]{1,0:T(8,128)S(1)} collective-permute-done((f32[1032,128]{1,0:T(8,128)S(1)}, f32[1032,128]{1,0:T(8,128)S(1)}, u32[]{:S(2)}, u32[]{:S(2)}) %collective-permute-start.13) | collective-permute-done | bytes 528416 | tf_op jit(solution)/shard_map/ppermute | solution.py:45
  45.7 0.1 collective-permute-start.14
  45.8 3.9 %collective-permute-done.12 = f32[1024,128]{1,0:T(8,128)S(1)} collective-permute-done((f32[1024,128]{1,0:T(8,128)S(1)}, f32[1024,128]{1,0:T(8,128)S(1)}, u32[]{:S(2)}, u32[]{:S(2)}) %collective-permute-start.12) | collective-permute-done | bytes 524320 | tf_op jit(solution)/shard_map/ppermute | solution.py:45
  49.8 3.7 %collective-permute-done.14 = f32[512,128]{1,0:T(8,128)S(1)} collective-permute-done((f32[512,128]{1,0:T(8,128)S(1)}, f32[512,128]{1,0:T(8,128)S(1)}, u32[]{:S(2)}, u32[]{:S(2)}) %collective-permute-start.14) | collective-permute-done | bytes 262176 | tf_op jit(solution)/shard_map/ppermute | solution.py:45
  53.5 0.1 add.26
  53.6 0.1 slice_add_fusion.1
  53.7 0.5 collective-permute-start.16
  54.2 5.2 %collective-permute-start.15 = (f32[256,128]{1,0:T(8,128)S(1)}, f32[256,128]{1,0:T(8,128)S(1)}, u32[]{:S(2)}, u32[]{:S(2)}) collective-permute-start(f32[256,128]{1,0:T(8,128)S(1)} %get-tuple-element.66), channel_id=1, source_target_pairs={{0,128},{1,5},{2,130},{3,7},{4,132},{5,1},{6,134},{7,3},{8,136},{9... | collective-permute-start | bytes 393224 | tf_op jit(solution)/shard_map/ppermute | solution.py:45
  59.4 0.0 collective-permute-start.17
  59.4 0.9 %collective-permute-done.16 = f32[256,128]{1,0:T(8,128)S(1)} collective-permute-done((f32[256,128]{1,0:T(8,128)S(1)}, f32[256,128]{1,0:T(8,128)S(1)}, u32[]{:S(2)}, u32[]{:S(2)}) %collective-permute-start.16) | collective-permute-done | bytes 131104 | tf_op jit(solution)/shard_map/ppermute | solution.py:45
  60.3 2.1 %collective-permute-done.15 = f32[256,128]{1,0:T(8,128)S(1)} collective-permute-done((f32[256,128]{1,0:T(8,128)S(1)}, f32[256,128]{1,0:T(8,128)S(1)}, u32[]{:S(2)}, u32[]{:S(2)}) %collective-permute-start.15) | collective-permute-done | bytes 131104 | tf_op jit(solution)/shard_map/ppermute | solution.py:45
  62.3 3.2 %collective-permute-done.17 = f32[256,128]{1,0:T(8,128)S(1)} collective-permute-done((f32[256,128]{1,0:T(8,128)S(1)}, f32[256,128]{1,0:T(8,128)S(1)}, u32[]{:S(2)}, u32[]{:S(2)}) %collective-permute-start.17) | collective-permute-done | bytes 131104 | tf_op jit(solution)/shard_map/ppermute | solution.py:45
  65.6 17.3 %all_to_all.5 = f32[8,32,128]{2,1,0:T(8,128)S(1)} all-to-all(f32[8,32,128]{2,1,0:T(8,128)S(1)} %bitcast.7), channel_id=1, replica_groups={{0,8,16,24,32,40,48,56},{64,72,80,88,96,104,112,120},{128,136,144,152,1..., dimensions={0} | all-to-all | bytes 262144 | tf_op jit(solution)/shard_map/all_to_all | solution.py:278
  82.9 0.6 reduce_sum.9
  (15 shorter events, 0.3 us)
Async XLA Ops:
  0.7 1.4 %copy-start = (f32[48,2,4096]{2,1,0:T(2,128)S(1)}, f32[48,2,4096]{2,1,0:T(2,128)}, u32[]{:S(2)}) copy-start(f32[48,2,4096]{2,1,0:T(2,128)} %param.4) | copy-start | bytes 4718596
  2.1 0.7 copy-start.1
  2.7 18.0 %copy-start.2 = (f32[128,1024]{1,0:T(8,128)S(1)}, f32[128,1024]{1,0:T(8,128)}, u32[]{:S(2)}) copy-start(f32[128,1024]{1,0:T(8,128)} %orbitals_ref.1) | copy-start | bytes 1572868
  3.6 9.4 %collective-permute-start.1 = (f32[392,128]{1,0:T(8,128)S(1)}, f32[392,128]{1,0:T(8,128)S(1)}, u32[]{:S(2)}, u32[]{:S(2)}) collective-permute-start(f32[392,128]{1,0:T(8,128)S(1)} %get-tuple-element.33), channel_id=1, source_target_pairs={{0,4},{1,5},{2,6},{3,7},{4,0},{5,1},{6,2},{7,3},{8,12},{9,13},{10,... | collective-permute-start | bytes 602120 | tf_op jit(solution)/shard_map/ppermute | solution.py:45
  6.8 13.3 %collective-permute-start.2 = (f32[392,128]{1,0:T(8,128)S(1)}, f32[392,128]{1,0:T(8,128)S(1)}, u32[]{:S(2)}, u32[]{:S(2)}) collective-permute-start(f32[392,128]{1,0:T(8,128)S(1)} %get-tuple-element.34), channel_id=1, source_target_pairs={{0,2},{1,3},{2,4},{3,5},{4,6},{5,7},{6,0},{7,1},{8,10},{9,11},{10,... | collective-permute-start | bytes 602120 | tf_op jit(solution)/shard_map/ppermute | solution.py:45
  7.4 12.7 %collective-permute-start.3 = (f32[392,128]{1,0:T(8,128)S(1)}, f32[392,128]{1,0:T(8,128)S(1)}, u32[]{:S(2)}, u32[]{:S(2)}) collective-permute-start(f32[392,128]{1,0:T(8,128)S(1)} %get-tuple-element.35), channel_id=1, source_target_pairs={{0,6},{1,7},{2,0},{3,1},{4,2},{5,3},{6,4},{7,5},{8,14},{9,15},{10,... | collective-permute-start | bytes 602120 | tf_op jit(solution)/shard_map/ppermute | solution.py:45
  10.0 15.7 %collective-permute-start.5 = (f32[384,128]{1,0:T(8,128)}, f32[384,128]{1,0:T(8,128)S(1)}, u32[]{:S(2)}, u32[]{:S(2)}) collective-permute-start(f32[384,128]{1,0:T(8,128)} %get-tuple-element.39), channel_id=1, source_target_pairs={{0,4},{1,5},{2,6},{3,7},{4,0},{5,1},{6,2},{7,3},{8,12},{9,13},{10,... | collective-permute-start | bytes 589832 | tf_op jit(solution)/shard_map/ppermute | solution.py:45
  10.0 15.7 %collective-permute-start.6 = (f32[384,128]{1,0:T(8,128)S(1)}, f32[384,128]{1,0:T(8,128)S(1)}, u32[]{:S(2)}, u32[]{:S(2)}) collective-permute-start(f32[384,128]{1,0:T(8,128)S(1)} %get-tuple-element.40), channel_id=1, source_target_pairs={{0,2},{1,3},{2,4},{3,5},{4,6},{5,7},{6,0},{7,1},{8,10},{9,11},{10,... | collective-permute-start | bytes 589832 | tf_op jit(solution)/shard_map/ppermute | solution.py:45
  12.9 12.7 %collective-permute-start.7 = (f32[384,128]{1,0:T(8,128)S(1)}, f32[384,128]{1,0:T(8,128)S(1)}, u32[]{:S(2)}, u32[]{:S(2)}) collective-permute-start(f32[384,128]{1,0:T(8,128)S(1)} %get-tuple-element.41), channel_id=1, source_target_pairs={{0,6},{1,7},{2,0},{3,1},{4,2},{5,3},{6,4},{7,5},{8,14},{9,15},{10,... | collective-permute-start | bytes 589832 | tf_op jit(solution)/shard_map/ppermute | solution.py:45
  20.1 1.7 %collective-permute-start = (f32[776,128]{1,0:T(8,128)S(1)}, f32[776,128]{1,0:T(8,128)S(1)}, u32[]{:S(2)}, u32[]{:S(2)}) collective-permute-start(f32[776,128]{1,0:T(8,128)S(1)} %get-tuple-element.32.own), channel_id=1, source_target_pairs={{0,1},{1,0},{2,3},{3,2},{4,5},{5,4},{6,7},{7,6},{8,9},{9,8},{10,11... | collective-permute-start | bytes 1191944 | tf_op jit(solution)/shard_map/ppermute | solution.py:45
  20.1 2.5 %collective-permute-start.4 = (f32[1176,128]{1,0:T(8,128)S(1)}, f32[1176,128]{1,0:T(8,128)S(1)}, u32[]{:S(2)}, u32[]{:S(2)}) collective-permute-start(f32[1176,128]{1,0:T(8,128)S(1)} %pad_maximum_fusion), channel_id=1, source_target_pairs={{0,1},{1,0},{2,3},{3,2},{4,5},{5,4},{6,7},{7,6},{8,9},{9,8},{10,11... | collective-permute-start | bytes 1806344 | tf_op jit(solution)/shard_map/ppermute | solution.py:45
  25.7 2.3 %collective-permute-start.8 = (f32[384,128]{1,0:T(8,128)S(1)}, f32[384,128]{1,0:T(8,128)S(1)}, u32[]{:S(2)}, u32[]{:S(2)}) collective-permute-start(f32[384,128]{1,0:T(8,128)S(1)} %collective-permute-done.5.refs_0_), channel_id=1, source_target_pairs={{0,1},{1,0},{2,3},{3,2},{4,5},{5,4},{6,7},{7,6},{8,9},{9,8},{10,11... | collective-permute-start | bytes 589832 | tf_op jit(solution)/shard_map/ppermute | solution.py:45
  25.9 2.1 %collective-permute-start.9 = (f32[384,128]{1,0:T(8,128)S(1)}, f32[384,128]{1,0:T(8,128)S(1)}, u32[]{:S(2)}, u32[]{:S(2)}) collective-permute-start(f32[384,128]{1,0:T(8,128)S(1)} %collective-permute-done.6.refs_1_), channel_id=1, source_target_pairs={{0,1},{1,0},{2,3},{3,2},{4,5},{5,4},{6,7},{7,6},{8,9},{9,8},{10,11... | collective-permute-start | bytes 589832 | tf_op jit(solution)/shard_map/ppermute | solution.py:45
  26.3 1.8 %collective-permute-start.10 = (f32[384,128]{1,0:T(8,128)S(1)}, f32[384,128]{1,0:T(8,128)S(1)}, u32[]{:S(2)}, u32[]{:S(2)}) collective-permute-start(f32[384,128]{1,0:T(8,128)S(1)} %collective-permute-done.7.refs_2_), channel_id=1, source_target_pairs={{0,1},{1,0},{2,3},{3,2},{4,5},{5,4},{6,7},{7,6},{8,9},{9,8},{10,11... | collective-permute-start | bytes 589832 | tf_op jit(solution)/shard_map/ppermute | solution.py:45
  32.4 6.8 %collective-permute-start.11 = (f32[520,128]{1,0:T(8,128)S(1)}, f32[520,128]{1,0:T(8,128)S(1)}, u32[]{:S(2)}, u32[]{:S(2)}) collective-permute-start(f32[520,128]{1,0:T(8,128)S(1)} %get-tuple-element.53), channel_id=1, source_target_pairs={{0,6},{1,193},{2,0},{3,195},{4,2},{5,197},{6,4},{7,199},{8,14},{9,... | collective-permute-start | bytes 798728 | tf_op jit(solution)/shard_map/ppermute | solution.py:45
  35.3 10.4 %collective-permute-start.13 = (f32[1032,128]{1,0:T(8,128)S(1)}, f32[1032,128]{1,0:T(8,128)S(1)}, u32[]{:S(2)}, u32[]{:S(2)}) collective-permute-start(f32[1032,128]{1,0:T(8,128)S(1)} %get-tuple-element.55), channel_id=1, source_target_pairs={{0,2},{1,65},{2,4},{3,67},{4,6},{5,69},{6,0},{7,71},{8,10},{9,73},... | collective-permute-start | bytes 1585160 | tf_op jit(solution)/shard_map/ppermute | solution.py:45
  39.3 10.5 %collective-permute-start.12 = (f32[1024,128]{1,0:T(8,128)S(1)}, f32[1024,128]{1,0:T(8,128)S(1)}, u32[]{:S(2)}, u32[]{:S(2)}) collective-permute-start(f32[1024,128]{1,0:T(8,128)S(1)} %pad_maximum_fusion.1), channel_id=1, source_target_pairs={{0,6},{1,193},{2,0},{3,195},{4,2},{5,197},{6,4},{7,199},{8,14},{9,... | collective-permute-start | bytes 1572872 | tf_op jit(solution)/shard_map/ppermute | solution.py:45
  45.7 7.7 %collective-permute-start.14 = (f32[512,128]{1,0:T(8,128)S(1)}, f32[512,128]{1,0:T(8,128)S(1)}, u32[]{:S(2)}, u32[]{:S(2)}) collective-permute-start(f32[512,128]{1,0:T(8,128)S(1)} %slice_add_fusion.2), channel_id=1, source_target_pairs={{0,2},{1,65},{2,4},{3,67},{4,6},{5,69},{6,0},{7,71},{8,10},{9,73},... | collective-permute-start | bytes 786440 | tf_op jit(solution)/shard_map/ppermute | solution.py:45
  53.7 6.6 %collective-permute-start.16 = (f32[256,128]{1,0:T(8,128)S(1)}, f32[256,128]{1,0:T(8,128)S(1)}, u32[]{:S(2)}, u32[]{:S(2)}) collective-permute-start(f32[256,128]{1,0:T(8,128)S(1)} %slice.94), channel_id=1, source_target_pairs={{0,64},{1,3},{2,66},{3,5},{4,68},{5,7},{6,70},{7,1},{8,72},{9,11},... | collective-permute-start | bytes 393224 | tf_op jit(solution)/shard_map/ppermute | solution.py:45
  54.2 8.2 %collective-permute-start.15 = (f32[256,128]{1,0:T(8,128)S(1)}, f32[256,128]{1,0:T(8,128)S(1)}, u32[]{:S(2)}, u32[]{:S(2)}) collective-permute-start(f32[256,128]{1,0:T(8,128)S(1)} %get-tuple-element.66), channel_id=1, source_target_pairs={{0,128},{1,5},{2,130},{3,7},{4,132},{5,1},{6,134},{7,3},{8,136},{9... | collective-permute-start | bytes 393224 | tf_op jit(solution)/shard_map/ppermute | solution.py:45
  59.4 6.2 %collective-permute-start.17 = (f32[256,128]{1,0:T(8,128)S(1)}, f32[256,128]{1,0:T(8,128)S(1)}, u32[]{:S(2)}, u32[]{:S(2)}) collective-permute-start(f32[256,128]{1,0:T(8,128)S(1)} %get-tuple-element.67), channel_id=1, source_target_pairs={{0,192},{1,7},{2,194},{3,1},{4,196},{5,3},{6,198},{7,5},{8,200},{9... | collective-permute-start | bytes 393224 | tf_op jit(solution)/shard_map/ppermute | solution.py:45

commit v5 on v3

--- a/solution.py
+++ b/solution.py
@@ -257,8 +257,9 @@
 
         return where
 
-    for part, k in ((one, 1), (three, 3), (two, 2)):
+    for part, k in ((one, 1), (three, 3)):
         summed += send(part, along(k, False))[:1024]
+    summed += jnp.concatenate([send(part, along(2, False)) for part in (two[:512], two[512:])])
     summed = summed.reshape(4, 256, 128)
     got = [send(summed[k], along(k, True)) for k in STEPS]
     summed = summed[0] + got[0] + got[1] + got[2]

time: 78.2 us -> 78.2 us (level)
    ppermute x17 -> x18, waiting for transfers between devices: 22.4 us -> 22 us  [send(): return lax.ppermute(array, ('aux', 'occ'), pairs)]
    ppermute x17 -> x18, starting transfers between devices: 22 us -> 22.4 us  [send(): return lax.ppermute(array, ('aux', 'occ'), pairs)]
  transfers between devices with their start and end apart: 17 -> 18, of which waited for: 9 -> 10; matrix products, arithmetic and copies ran while one was open for 0% -> 0% of each run, Pallas kernels for 9% -> 9%
where the time goes in v5:
time: 78.2 us; the launch traced here: 78 us
  starting transfers between devices  22.4 us (29%)
  waiting for transfers between devices  22 us (28%)
  blocking collectives  17.3 us (22%)
  Pallas kernels  12.4 us (16%)
  local copies, waits for them, and re-layouts  2.26 us (3%)
  other arithmetic  0.86 us (1%)
  between operations  0.82 us (1%)
    ppermute x18, starting transfers between devices, send(): return lax.ppermute(array, ('aux', 'occ'), pairs)  22.4 us
    ppermute x18, waiting for transfers between devices, send(): return lax.ppermute(array, ('aux', 'occ'), pairs)  22 us
    all_to_all x1, blocking collectives, per_device(): lax.all_to_all(summed.reshape(NZ, 32, 128), 'aux', 0, 0, axis_index_group...  17.3 us
    pallas_call x2, Pallas kernels, half(): call(functools.partial(half_kernel, chunk), [shape((NBF, count * NOCC), B...  5.69 us
    pallas_call x3, Pallas kernels, partial(): call(functools.partial(exchange_kernel, steps, len(halves) // 2), [shape(...  5.68 us
    unnamed x6, local copies, waits for them, and re-layouts  2.08 us
  transfers between devices with their start and end apart: 18, of which 10 were waited for; matrix products, arithmetic and copies ran while one was open for 0% of the time, Pallas kernels for 9%

profile of v5, /device:TPU:8, one launch (start us, length us, event | category | flops | bytes accessed | tf_op | source)
XLA Modules:
  0.0 78.0 jit_solution(3037708180386383658)
XLA Ops:
  0.7 0.0 copy-start
  0.7 1.4 %copy-done = f32[48,2,4096]{2,1,0:T(2,128)S(1)} copy-done((f32[48,2,4096]{2,1,0:T(2,128)S(1)}, f32[48,2,4096]{2,1,0:T(2,128)}, u32[]{:S(2)}) %copy-start) | copy-done | bytes 1572888
  2.1 0.0 copy-start.1
  2.1 0.7 copy-done.1
  2.7 0.0 copy-start.2
  2.7 0.8 %shard_map.46 = (f32[776,128]{1,0:T(8,128)S(1)}, f32[392,128]{1,0:T(8,128)S(1)}, f32[392,128]{1,0:T(8,128)S(1)}, f32[392,128]{1,0:T(8,128)S(1)}, f32[384,128]{1,...) custom-call(s32[1,2,2]{2,1,0:T(2,128)S(1)} %copy-done.1, s32[1]{0:T(128)S(6)} %copy.5.count_ref, ...), custom_call_target="tpu_custom_call" | custom-call | tf_op jit(solution)/shard_map/pallas_call | solution.py:202
  3.6 2.3 %collective-permute-start.1 = (f32[392,128]{1,0:T(8,128)S(1)}, f32[392,128]{1,0:T(8,128)S(1)}, u32[]{:S(2)}, u32[]{:S(2)}) collective-permute-start(f32[392,128]{1,0:T(8,128)S(1)} %get-tuple-element.29), channel_id=1, source_target_pairs={{0,4},{1,5},{2,6},{3,7},{4,0},{5,1},{6,2},{7,3},{8,12},{9,13},{10,... | collective-permute-start | bytes 602120 | tf_op jit(solution)/shard_map/ppermute | solution.py:41
  5.9 1.4 %collective-permute-start.2 = (f32[392,128]{1,0:T(8,128)S(1)}, f32[392,128]{1,0:T(8,128)S(1)}, u32[]{:S(2)}, u32[]{:S(2)}) collective-permute-start(f32[392,128]{1,0:T(8,128)S(1)} %get-tuple-element.30), channel_id=1, source_target_pairs={{0,2},{1,3},{2,4},{3,5},{4,6},{5,7},{6,0},{7,1},{8,10},{9,11},{10,... | collective-permute-start | bytes 602120 | tf_op jit(solution)/shard_map/ppermute | solution.py:41
  7.2 0.7 collective-permute-start.3
  7.9 1.4 %collective-permute-start.5 = (f32[384,128]{1,0:T(8,128)}, f32[384,128]{1,0:T(8,128)S(1)}, u32[]{:S(2)}, u32[]{:S(2)}) collective-permute-start(f32[384,128]{1,0:T(8,128)} %get-tuple-element.35), channel_id=1, source_target_pairs={{0,4},{1,5},{2,6},{3,7},{4,0},{5,1},{6,2},{7,3},{8,12},{9,13},{10,... | collective-permute-start | bytes 589832 | tf_op jit(solution)/shard_map/ppermute | solution.py:41
  9.3 2.6 %collective-permute-start.6 = (f32[384,128]{1,0:T(8,128)S(1)}, f32[384,128]{1,0:T(8,128)S(1)}, u32[]{:S(2)}, u32[]{:S(2)}) collective-permute-start(f32[384,128]{1,0:T(8,128)S(1)} %get-tuple-element.36), channel_id=1, source_target_pairs={{0,2},{1,3},{2,4},{3,5},{4,6},{5,7},{6,0},{7,1},{8,10},{9,11},{10,... | collective-permute-start | bytes 589832 | tf_op jit(solution)/shard_map/ppermute | solution.py:41
  11.9 1.1 %collective-permute-done.1.refs_0_ = f32[392,128]{1,0:T(8,128)S(1)} collective-permute-done((f32[392,128]{1,0:T(8,128)S(1)}, f32[392,128]{1,0:T(8,128)S(1)}, u32[]{:S(2)}, u32[]{:S(2)}) %collective-permute-start.1) | collective-permute-done | bytes 200736 | tf_op jit(solution)/shard_map/ppermute | solution.py:41
  13.0 2.0 %collective-permute-start.7 = (f32[384,128]{1,0:T(8,128)S(1)}, f32[384,128]{1,0:T(8,128)S(1)}, u32[]{:S(2)}, u32[]{:S(2)}) collective-permute-start(f32[384,128]{1,0:T(8,128)S(1)} %get-tuple-element.37), channel_id=1, source_target_pairs={{0,6},{1,7},{2,0},{3,1},{4,2},{5,3},{6,4},{7,5},{8,14},{9,15},{10,... | collective-permute-start | bytes 589832 | tf_op jit(solution)/shard_map/ppermute | solution.py:41
  15.0 2.4 %collective-permute-done.2.refs_1_ = f32[392,128]{1,0:T(8,128)S(1)} collective-permute-done((f32[392,128]{1,0:T(8,128)S(1)}, f32[392,128]{1,0:T(8,128)S(1)}, u32[]{:S(2)}, u32[]{:S(2)}) %collective-permute-start.2) | collective-permute-done | bytes 200736 | tf_op jit(solution)/shard_map/ppermute | solution.py:41
  17.4 0.0 collective-permute-start
  17.4 0.0 collective-permute-done.3.refs_2_
  17.4 0.6 collective-permute-start.4
  18.0 0.0 copy-done.2
  18.0 0.2 shard_map.47
  18.3 0.8 %collective-permute-done.own_other = f32[776,128]{1,0:T(8,128)S(1)} collective-permute-done((f32[776,128]{1,0:T(8,128)S(1)}, f32[776,128]{1,0:T(8,128)S(1)}, u32[]{:S(2)}, u32[]{:S(2)}) %collective-permute-start) | collective-permute-done | bytes 397344 | tf_op jit(solution)/shard_map/ppermute | solution.py:41
  19.1 0.9 %collective-permute-done.4.refs_3_ = f32[1176,128]{1,0:T(8,128)S(1)} collective-permute-done((f32[1176,128]{1,0:T(8,128)S(1)}, f32[1176,128]{1,0:T(8,128)S(1)}, u32[]{:S(2)}, u32[]{:S(2)}) %collective-permute-start.4) | collective-permute-done | bytes 602144 | tf_op jit(solution)/shard_map/ppermute | solution.py:41
  20.0 0.1 reshape.23.info_ref
  20.1 2.8 %shard_map.48 = (bf16[1024,768]{1,0:T(8,128)(2,1)S(1)}, bf16[1024,768]{1,0:T(8,128)(2,1)S(1)}) custom-call(s32[16,3]{1,0:T(8,128)S(1)} %reshape.23.info_ref, bf16[1024,128]{1,0:T(8,128)(2,1)S(1)} %get-tuple-element.32.high_t, bf16[1024,128]{1,0:T(8,128)(2,1)S(1)} %get-tuple-element.33.low_t, f32[776,128]{1,0:T(8,128)S(1)} %get-tuple-element.28.own, ...), custom_call_target="tpu_custom_call" | custom-call | tf_op jit(solution)/shard_map/pallas_call | solution.py:232
  22.9 0.0 collective-permute-done.5.refs_0_
  22.9 1.8 %collective-permute-done.6.refs_1_ = f32[384,128]{1,0:T(8,128)S(1)} collective-permute-done((f32[384,128]{1,0:T(8,128)S(1)}, f32[384,128]{1,0:T(8,128)S(1)}, u32[]{:S(2)}, u32[]{:S(2)}) %collective-permute-start.6) | collective-permute-done | bytes 196640 | tf_op jit(solution)/shard_map/ppermute | solution.py:41
  24.7 0.0 collective-permute-done.7.refs_2_
  24.7 0.0 collective-permute-start.8
  24.7 0.5 collective-permute-start.9
  25.2 0.0 collective-permute-start.10
  25.3 1.6 %shard_map.51 = (f32[1032,128]{1,0:T(8,128)S(1)}, f32[1032,128]{1,0:T(8,128)S(1)}) custom-call(bf16[1024,768]{1,0:T(8,128)(2,1)S(1)} %get-tuple-element.38.refs_0_, bf16[1024,768]{1,0:T(8,128)(2,1)S(1)} %get-tuple-element.39.refs_1_), custom_call_target="tpu_custom_call" | custom-call | flops 2415919104 | tf_op jit(solution)/shard_map/pallas_call | solution.py:240
  26.9 0.0 collective-permute-done.8.refs_3_
  26.9 0.0 collective-permute-done.9.refs_4_
  26.9 0.0 collective-permute-done.10.refs_5_
  26.9 2.8 %shard_map.49 = (bf16[1024,768]{1,0:T(8,128)(2,1)S(1)}, bf16[1024,768]{1,0:T(8,128)(2,1)S(1)}) custom-call(s32[16,3]{1,0:T(8,128)S(1)} %reshape.23.info_ref, bf16[1024,128]{1,0:T(8,128)(2,1)S(1)} %get-tuple-element.32.high_t, bf16[1024,128]{1,0:T(8,128)(2,1)S(1)} %get-tuple-element.33.low_t, f32[776,128]{1,0:T(8,128)S(1)} %get-tuple-element.28.own, ...), custom_call_target="tpu_custom_call" | custom-call | tf_op jit(solution)/shard_map/pallas_call | solution.py:232
  29.7 1.5 %shard_map.52 = (f32[1032,128]{1,0:T(8,128)S(1)}, f32[1032,128]{1,0:T(8,128)S(1)}) custom-call(bf16[1024,768]{1,0:T(8,128)(2,1)S(1)} %get-tuple-element.43.refs_2_.refs_0_, bf16[1024,768]{1,0:T(8,128)(2,1)S(1)} %get-tuple-element.44.refs_3_.refs_1_, f32[1032,128]{1,0:T(8,128)S(1)} %get-tuple-element.46.refs_2_, f32[1032,128]{1,0:T(8,128)S(1)} %get-tuple-element.47.refs_3_), custom_call_target="tpu_custom_call" | custom-call | flops 2415919104 | tf_op jit(solution)/shard_map/pallas_call | solution.py:240
  31.2 2.2 %collective-permute-start.11 = (f32[1032,128]{1,0:T(8,128)S(1)}, f32[1032,128]{1,0:T(8,128)S(1)}, u32[]{:S(2)}, u32[]{:S(2)}) collective-permute-start(f32[1032,128]{1,0:T(8,128)S(1)} %get-tuple-element.48), channel_id=1, source_target_pairs={{0,2},{1,65},{2,4},{3,67},{4,6},{5,69},{6,0},{7,71},{8,10},{9,73},... | collective-permute-start | bytes 1585160 | tf_op jit(solution)/shard_map/ppermute | solution.py:41
  33.4 0.0 collective-permute-start.12
  33.4 2.6 %shard_map.50 = (f32[1024,128]{1,0:T(8,128)S(1)}, f32[1024,128]{1,0:T(8,128)S(1)}) custom-call(bf16[1024,768]{1,0:T(8,128)(2,1)S(1)} %get-tuple-element.38.refs_0_, bf16[1024,768]{1,0:T(8,128)(2,1)S(1)} %get-tuple-element.39.refs_1_, bf16[1024,768]{1,0:T(8,128)(2,1)S(1)} %get-tuple-element.43.refs_2_.refs_0_, ...), custom_call_target="tpu_custom_call" | custom-call | flops 2415919104 | tf_op jit(solution)/shard_map/pallas_call | solution.py:240
  36.1 3.3 %collective-permute-start.13 = (f32[512,128]{1,0:T(8,128)S(1)}, f32[512,128]{1,0:T(8,128)S(1)}, u32[]{:S(2)}, u32[]{:S(2)}) collective-permute-start(f32[512,128]{1,0:T(8,128)S(1)} %get-tuple-element.57), channel_id=1, source_target_pairs={{0,4},{1,129},{2,6},{3,131},{4,0},{5,133},{6,2},{7,135},{8,12},{9,... | collective-permute-start | bytes 786440 | tf_op jit(solution)/shard_map/ppermute | solution.py:41
  39.4 0.3 collective-permute-start.14
  39.7 6.9 %collective-permute-done.13 = f32[512,128]{1,0:T(8,128)S(1)} collective-permute-done((f32[512,128]{1,0:T(8,128)S(1)}, f32[512,128]{1,0:T(8,128)S(1)}, u32[]{:S(2)}, u32[]{:S(2)}) %collective-permute-start.13) | collective-permute-done | bytes 262176 | tf_op jit(solution)/shard_map/ppermute | solution.py:41
  46.6 2.8 %collective-permute-done.14 = f32[512,128]{1,0:T(8,128)S(1)} collective-permute-done((f32[512,128]{1,0:T(8,128)S(1)}, f32[512,128]{1,0:T(8,128)S(1)}, u32[]{:S(2)}, u32[]{:S(2)}) %collective-permute-start.14) | collective-permute-done | bytes 262176 | tf_op jit(solution)/shard_map/ppermute | solution.py:41
  49.4 0.0 collective-permute-done.11
  49.4 0.0 collective-permute-done.12
  49.4 0.2 fusion
  49.6 3.1 %collective-permute-start.15 = (f32[256,128]{1,0:T(8,128)S(1)}, f32[256,128]{1,0:T(8,128)S(1)}, u32[]{:S(2)}, u32[]{:S(2)}) collective-permute-start(f32[256,128]{1,0:T(8,128)S(1)} %get-tuple-element.54), channel_id=1, source_target_pairs={{0,128},{1,5},{2,130},{3,7},{4,132},{5,1},{6,134},{7,3},{8,136},{9... | collective-permute-start | bytes 393224 | tf_op jit(solution)/shard_map/ppermute | solution.py:41
  52.7 1.1 %collective-permute-start.17 = (f32[256,128]{1,0:T(8,128)S(1)}, f32[256,128]{1,0:T(8,128)S(1)}, u32[]{:S(2)}, u32[]{:S(2)}) collective-permute-start(f32[256,128]{1,0:T(8,128)S(1)} %get-tuple-element.55), channel_id=1, source_target_pairs={{0,192},{1,7},{2,194},{3,1},{4,196},{5,3},{6,198},{7,5},{8,200},{9... | collective-permute-start | bytes 393224 | tf_op jit(solution)/shard_map/ppermute | solution.py:41
  53.9 0.9 %collective-permute-start.16 = (f32[256,128]{1,0:T(8,128)S(1)}, f32[256,128]{1,0:T(8,128)S(1)}, u32[]{:S(2)}, u32[]{:S(2)}) collective-permute-start(f32[256,128]{1,0:T(8,128)S(1)} %get-tuple-element.56), channel_id=1, source_target_pairs={{0,64},{1,3},{2,66},{3,5},{4,68},{5,7},{6,70},{7,1},{8,72},{9,11},... | collective-permute-start | bytes 393224 | tf_op jit(solution)/shard_map/ppermute | solution.py:41
  54.7 1.4 %collective-permute-done.15 = f32[256,128]{1,0:T(8,128)S(1)} collective-permute-done((f32[256,128]{1,0:T(8,128)S(1)}, f32[256,128]{1,0:T(8,128)S(1)}, u32[]{:S(2)}, u32[]{:S(2)}) %collective-permute-start.15) | collective-permute-done | bytes 131104 | tf_op jit(solution)/shard_map/ppermute | solution.py:41
  56.2 1.5 %collective-permute-done.17 = f32[256,128]{1,0:T(8,128)S(1)} collective-permute-done((f32[256,128]{1,0:T(8,128)S(1)}, f32[256,128]{1,0:T(8,128)S(1)}, u32[]{:S(2)}, u32[]{:S(2)}) %collective-permute-start.17) | collective-permute-done | bytes 131104 | tf_op jit(solution)/shard_map/ppermute | solution.py:41
  57.7 2.3 %collective-permute-done.16 = f32[256,128]{1,0:T(8,128)S(1)} collective-permute-done((f32[256,128]{1,0:T(8,128)S(1)}, f32[256,128]{1,0:T(8,128)S(1)}, u32[]{:S(2)}, u32[]{:S(2)}) %collective-permute-start.16) | collective-permute-done | bytes 131104 | tf_op jit(solution)/shard_map/ppermute | solution.py:41
  60.1 17.3 %all_to_all.5 = f32[8,32,128]{2,1,0:T(8,128)S(1)} all-to-all(f32[8,32,128]{2,1,0:T(8,128)S(1)} %bitcast.7), channel_id=1, replica_groups={{0,8,16,24,32,40,48,56},{64,72,80,88,96,104,112,120},{128,136,144,152,1..., dimensions={0} | all-to-all | bytes 262144 | tf_op jit(solution)/shard_map/all_to_all | solution.py:267
  77.4 0.6 reduce_sum.9
  (12 shorter events, 0.2 us)
Async XLA Ops:
  0.7 1.4 %copy-start = (f32[48,2,4096]{2,1,0:T(2,128)S(1)}, f32[48,2,4096]{2,1,0:T(2,128)}, u32[]{:S(2)}) copy-start(f32[48,2,4096]{2,1,0:T(2,128)} %param.4) | copy-start | bytes 4718596
  2.1 0.7 copy-start.1
  2.7 15.3 %copy-start.2 = (f32[128,1024]{1,0:T(8,128)S(1)}, f32[128,1024]{1,0:T(8,128)}, u32[]{:S(2)}) copy-start(f32[128,1024]{1,0:T(8,128)} %orbitals_ref.1) | copy-start | bytes 1572868
  3.6 9.4 %collective-permute-start.1 = (f32[392,128]{1,0:T(8,128)S(1)}, f32[392,128]{1,0:T(8,128)S(1)}, u32[]{:S(2)}, u32[]{:S(2)}) collective-permute-start(f32[392,128]{1,0:T(8,128)S(1)} %get-tuple-element.29), channel_id=1, source_target_pairs={{0,4},{1,5},{2,6},{3,7},{4,0},{5,1},{6,2},{7,3},{8,12},{9,13},{10,... | collective-permute-start | bytes 602120 | tf_op jit(solution)/shard_map/ppermute | solution.py:41
  5.9 11.5 %collective-permute-start.2 = (f32[392,128]{1,0:T(8,128)S(1)}, f32[392,128]{1,0:T(8,128)S(1)}, u32[]{:S(2)}, u32[]{:S(2)}) collective-permute-start(f32[392,128]{1,0:T(8,128)S(1)} %get-tuple-element.30), channel_id=1, source_target_pairs={{0,2},{1,3},{2,4},{3,5},{4,6},{5,7},{6,0},{7,1},{8,10},{9,11},{10,... | collective-permute-start | bytes 602120 | tf_op jit(solution)/shard_map/ppermute | solution.py:41
  7.2 10.2 %collective-permute-start.3 = (f32[392,128]{1,0:T(8,128)S(1)}, f32[392,128]{1,0:T(8,128)S(1)}, u32[]{:S(2)}, u32[]{:S(2)}) collective-permute-start(f32[392,128]{1,0:T(8,128)S(1)} %get-tuple-element.31), channel_id=1, source_target_pairs={{0,6},{1,7},{2,0},{3,1},{4,2},{5,3},{6,4},{7,5},{8,14},{9,15},{10,... | collective-permute-start | bytes 602120 | tf_op jit(solution)/shard_map/ppermute | solution.py:41
  7.9 15.0 %collective-permute-start.5 = (f32[384,128]{1,0:T(8,128)}, f32[384,128]{1,0:T(8,128)S(1)}, u32[]{:S(2)}, u32[]{:S(2)}) collective-permute-start(f32[384,128]{1,0:T(8,128)} %get-tuple-element.35), channel_id=1, source_target_pairs={{0,4},{1,5},{2,6},{3,7},{4,0},{5,1},{6,2},{7,3},{8,12},{9,13},{10,... | collective-permute-start | bytes 589832 | tf_op jit(solution)/shard_map/ppermute | solution.py:41
  9.3 15.4 %collective-permute-start.6 = (f32[384,128]{1,0:T(8,128)S(1)}, f32[384,128]{1,0:T(8,128)S(1)}, u32[]{:S(2)}, u32[]{:S(2)}) collective-permute-start(f32[384,128]{1,0:T(8,128)S(1)} %get-tuple-element.36), channel_id=1, source_target_pairs={{0,2},{1,3},{2,4},{3,5},{4,6},{5,7},{6,0},{7,1},{8,10},{9,11},{10,... | collective-permute-start | bytes 589832 | tf_op jit(solution)/shard_map/ppermute | solution.py:41
  13.0 11.7 %collective-permute-start.7 = (f32[384,128]{1,0:T(8,128)S(1)}, f32[384,128]{1,0:T(8,128)S(1)}, u32[]{:S(2)}, u32[]{:S(2)}) collective-permute-start(f32[384,128]{1,0:T(8,128)S(1)} %get-tuple-element.37), channel_id=1, source_target_pairs={{0,6},{1,7},{2,0},{3,1},{4,2},{5,3},{6,4},{7,5},{8,14},{9,15},{10,... | collective-permute-start | bytes 589832 | tf_op jit(solution)/shard_map/ppermute | solution.py:41
  17.4 1.7 %collective-permute-start = (f32[776,128]{1,0:T(8,128)S(1)}, f32[776,128]{1,0:T(8,128)S(1)}, u32[]{:S(2)}, u32[]{:S(2)}) collective-permute-start(f32[776,128]{1,0:T(8,128)S(1)} %get-tuple-element.28.own), channel_id=1, source_target_pairs={{0,1},{1,0},{2,3},{3,2},{4,5},{5,4},{6,7},{7,6},{8,9},{9,8},{10,11... | collective-permute-start | bytes 1191944 | tf_op jit(solution)/shard_map/ppermute | solution.py:41
  17.4 2.5 %collective-permute-start.4 = (f32[1176,128]{1,0:T(8,128)S(1)}, f32[1176,128]{1,0:T(8,128)S(1)}, u32[]{:S(2)}, u32[]{:S(2)}) collective-permute-start(f32[1176,128]{1,0:T(8,128)S(1)} %pad_maximum_fusion), channel_id=1, source_target_pairs={{0,1},{1,0},{2,3},{3,2},{4,5},{5,4},{6,7},{7,6},{8,9},{9,8},{10,11... | collective-permute-start | bytes 1806344 | tf_op jit(solution)/shard_map/ppermute | solution.py:41
  24.7 2.1 %collective-permute-start.8 = (f32[384,128]{1,0:T(8,128)S(1)}, f32[384,128]{1,0:T(8,128)S(1)}, u32[]{:S(2)}, u32[]{:S(2)}) collective-permute-start(f32[384,128]{1,0:T(8,128)S(1)} %collective-permute-done.5.refs_0_), channel_id=1, source_target_pairs={{0,1},{1,0},{2,3},{3,2},{4,5},{5,4},{6,7},{7,6},{8,9},{9,8},{10,11... | collective-permute-start | bytes 589832 | tf_op jit(solution)/shard_map/ppermute | solution.py:41
  24.7 2.1 %collective-permute-start.9 = (f32[384,128]{1,0:T(8,128)S(1)}, f32[384,128]{1,0:T(8,128)S(1)}, u32[]{:S(2)}, u32[]{:S(2)}) collective-permute-start(f32[384,128]{1,0:T(8,128)S(1)} %collective-permute-done.6.refs_1_), channel_id=1, source_target_pairs={{0,1},{1,0},{2,3},{3,2},{4,5},{5,4},{6,7},{7,6},{8,9},{9,8},{10,11... | collective-permute-start | bytes 589832 | tf_op jit(solution)/shard_map/ppermute | solution.py:41
  25.2 1.6 %collective-permute-start.10 = (f32[384,128]{1,0:T(8,128)S(1)}, f32[384,128]{1,0:T(8,128)S(1)}, u32[]{:S(2)}, u32[]{:S(2)}) collective-permute-start(f32[384,128]{1,0:T(8,128)S(1)} %collective-permute-done.7.refs_2_), channel_id=1, source_target_pairs={{0,1},{1,0},{2,3},{3,2},{4,5},{5,4},{6,7},{7,6},{8,9},{9,8},{10,11... | collective-permute-start | bytes 589832 | tf_op jit(solution)/shard_map/ppermute | solution.py:41
  31.2 18.2 %collective-permute-start.11 = (f32[1032,128]{1,0:T(8,128)S(1)}, f32[1032,128]{1,0:T(8,128)S(1)}, u32[]{:S(2)}, u32[]{:S(2)}) collective-permute-start(f32[1032,128]{1,0:T(8,128)S(1)} %get-tuple-element.48), channel_id=1, source_target_pairs={{0,2},{1,65},{2,4},{3,67},{4,6},{5,69},{6,0},{7,71},{8,10},{9,73},... | collective-permute-start | bytes 1585160 | tf_op jit(solution)/shard_map/ppermute | solution.py:41
  33.4 16.0 %collective-permute-start.12 = (f32[1032,128]{1,0:T(8,128)S(1)}, f32[1032,128]{1,0:T(8,128)S(1)}, u32[]{:S(2)}, u32[]{:S(2)}) collective-permute-start(f32[1032,128]{1,0:T(8,128)S(1)} %get-tuple-element.49), channel_id=1, source_target_pairs={{0,6},{1,193},{2,0},{3,195},{4,2},{5,197},{6,4},{7,199},{8,14},{9,... | collective-permute-start | bytes 1585160 | tf_op jit(solution)/shard_map/ppermute | solution.py:41
  36.1 10.5 %collective-permute-start.13 = (f32[512,128]{1,0:T(8,128)S(1)}, f32[512,128]{1,0:T(8,128)S(1)}, u32[]{:S(2)}, u32[]{:S(2)}) collective-permute-start(f32[512,128]{1,0:T(8,128)S(1)} %get-tuple-element.57), channel_id=1, source_target_pairs={{0,4},{1,129},{2,6},{3,131},{4,0},{5,133},{6,2},{7,135},{8,12},{9,... | collective-permute-start | bytes 786440 | tf_op jit(solution)/shard_map/ppermute | solution.py:41
  39.4 10.1 %collective-permute-start.14 = (f32[512,128]{1,0:T(8,128)S(1)}, f32[512,128]{1,0:T(8,128)S(1)}, u32[]{:S(2)}, u32[]{:S(2)}) collective-permute-start(f32[512,128]{1,0:T(8,128)S(1)} %get-tuple-element.58), channel_id=1, source_target_pairs={{0,4},{1,129},{2,6},{3,131},{4,0},{5,133},{6,2},{7,135},{8,12},{9,... | collective-permute-start | bytes 786440 | tf_op jit(solution)/shard_map/ppermute | solution.py:41
  49.6 6.6 %collective-permute-start.15 = (f32[256,128]{1,0:T(8,128)S(1)}, f32[256,128]{1,0:T(8,128)S(1)}, u32[]{:S(2)}, u32[]{:S(2)}) collective-permute-start(f32[256,128]{1,0:T(8,128)S(1)} %get-tuple-element.54), channel_id=1, source_target_pairs={{0,128},{1,5},{2,130},{3,7},{4,132},{5,1},{6,134},{7,3},{8,136},{9... | collective-permute-start | bytes 393224 | tf_op jit(solution)/shard_map/ppermute | solution.py:41
  52.7 5.0 %collective-permute-start.17 = (f32[256,128]{1,0:T(8,128)S(1)}, f32[256,128]{1,0:T(8,128)S(1)}, u32[]{:S(2)}, u32[]{:S(2)}) collective-permute-start(f32[256,128]{1,0:T(8,128)S(1)} %get-tuple-element.55), channel_id=1, source_target_pairs={{0,192},{1,7},{2,194},{3,1},{4,196},{5,3},{6,198},{7,5},{8,200},{9... | collective-permute-start | bytes 393224 | tf_op jit(solution)/shard_map/ppermute | solution.py:41
  53.9 6.2 %collective-permute-start.16 = (f32[256,128]{1,0:T(8,128)S(1)}, f32[256,128]{1,0:T(8,128)S(1)}, u32[]{:S(2)}, u32[]{:S(2)}) collective-permute-start(f32[256,128]{1,0:T(8,128)S(1)} %get-tuple-element.56), channel_id=1, source_target_pairs={{0,64},{1,3},{2,66},{3,5},{4,68},{5,7},{6,70},{7,1},{8,72},{9,11},... | collective-permute-start | bytes 393224 | tf_op jit(solution)/shard_map/ppermute | solution.py:41
